TPU v7x, 768 devices: a whole 4x8x12 slice. The times are simulated.
768 devices in a mesh: group: 16 (over z_hi, x, core), shard: 48 (over y, z_lo).
Axes of the slice: x: 4, y: 8, z: 12 (z_hi: 2, z_lo: 6; z = z_hi * 6 + z_lo), core: 2. Of those that a mesh axis runs over, the one named last changes fastest.
Arguments:
- table: float32 [16, 48, 1024, 256], P('group', 'shard'), may hold values from -0.6 to 0.6
- row_state: float32 [16, 48, 1024], P('group', 'shard'), may hold values from 0.1 to 1
- bag_ids: int32 [16, 48, 4, 1536], P('group', 'shard'), may hold values from 0 to 1023
- bag_lengths: int32 [16, 48, 1536], P('group', 'shard'), may hold values from 1 to 4, as said below
- interaction_grad: float32 [16, 48, 48, 1536], P('group', None, None, 'shard'), may hold values from -0.875 to 0.875
- move_rows: int32 [16, 48, 16], P('group', 'shard'), may hold values from 0 to 64, as said below
Outputs:
- new_table: float32 [16, 48, 1024, 256], P('group', 'shard')
- new_state: float32 [16, 48, 1024], P('group', 'shard')
- arrived: float32 [16, 16, 48, 64, 256], P('group', None, 'shard')
- arrived_state: float32 [16, 16, 48, 64], P('group', None, 'shard')
Inputs may be any that keep to these rules, and one draw needn't show every extreme that they name: `bag_lengths`: in every table shard some bag has exactly 4 live slots. `move_rows`: every table shard sends exactly 64 rows to at least one group; its rows sent add up to at most 1024.
All inputs are finite; a program needn't handle non-finite values.
Results may differ from a plain program's by a relative error of at most 0.0009.
Values may be sent and summed in bfloat16 or wider, within the bound.
A program may use at most 32 MiB of HBM per device.

v0:
```python
import jax
import jax.numpy as jnp
from jax import lax
from jax.sharding import PartitionSpec as P

CAP = 64


learn_rate = 0.05
epsilon = 1e-08


def pool_table(rows_table, bag_rows, bag_len):

    def pool_add_slot(bag_slot, running):
        picked = rows_table[bag_rows[bag_slot]]
        return running + jnp.where((bag_slot < bag_len)[:, None], picked, 0.0)

    initial = jnp.zeros((bag_rows.shape[1], rows_table.shape[1]), jnp.float32)
    return lax.fori_loop(0, bag_rows.shape[0], pool_add_slot, initial)


def row_gradients(num_rows, bag_rows, bag_len, upstream_rows):
    grad_values = upstream_rows.astype(jnp.float32)

    def row_add_slot(bag_slot, running):
        masked = jnp.where((bag_slot < bag_len)[:, None], grad_values, 0.0)
        return running.at[bag_rows[bag_slot]].add(masked)

    initial = jnp.zeros((num_rows, upstream_rows.shape[1]), jnp.float32)
    return lax.fori_loop(0, bag_rows.shape[0], row_add_slot, initial)


def slot_layout(counts, num_rows):
    starts = jnp.cumsum(counts) - counts
    offsets = jnp.arange(CAP, dtype=jnp.int32)
    slot_rows = jnp.clip(starts[:, None] + offsets[None, :], 0, num_rows - 1)
    live_slots = offsets[None, :] < counts[:, None]
    return (slot_rows, live_slots)


def on_device(table, row_state, bag_ids, bag_lengths, interaction_grad, move_rows):
    rows_table = table[0, 0]
    state_rows = row_state[0, 0]
    bag_rows = bag_ids[0, 0]
    bag_len = bag_lengths[0, 0]
    counts = move_rows[0, 0]
    grad_block = interaction_grad[0]
    shards = lax.axis_size("shard")
    groups = lax.axis_size("group")
    samples = bag_rows.shape[1]
    per_shard = samples // shards
    row_width = rows_table.shape[1]
    num_rows = rows_table.shape[0]
    slot_rows, live_slots = slot_layout(counts, num_rows)
    pooled = pool_table(rows_table, bag_rows, bag_len).astype(jnp.bfloat16)
    received = lax.all_to_all(
        pooled.reshape(1, shards, per_shard, row_width),
        "shard",
        split_axis=1,
        concat_axis=0,
        tiled=True,
    )
    received = received.reshape(shards, per_shard, row_width)
    symmetric = grad_block + jnp.transpose(grad_block, (1, 0, 2))
    upstream = jnp.einsum(
        "fgb,gbe->fbe", symmetric, received.astype(jnp.float32), precision=lax.Precision.HIGHEST
    ).astype(jnp.bfloat16)
    returned = lax.all_to_all(
        upstream.reshape(shards, 1, per_shard, row_width),
        "shard",
        split_axis=0,
        concat_axis=1,
        tiled=True,
    )
    returned = returned.reshape(samples, row_width)
    row_grads = row_gradients(num_rows, bag_rows, bag_len, returned)
    new_state = state_rows + jnp.mean(row_grads * row_grads, axis=-1)
    new_rows = rows_table - learn_rate * row_grads / (jnp.sqrt(new_state)[:, None] + epsilon)
    moved_rows = jnp.where(live_slots[..., None], new_rows[slot_rows], 0.0)
    moved_state = jnp.where(live_slots, new_state[slot_rows], 0.0)
    arrived, arrived_state = (
        lax.all_to_all(moved_rows, "group", split_axis=0, concat_axis=0, tiled=True),
        lax.all_to_all(moved_state, "group", split_axis=0, concat_axis=0, tiled=True),
    )
    return (
        new_rows[None, None],
        new_state[None, None],
        arrived.reshape(1, groups, 1, CAP, row_width),
        arrived_state.reshape(1, groups, 1, CAP),
    )


def solution(mesh):
    in_specs = (
        P("group", "shard", None, None),
        P("group", "shard", None),
        P("group", "shard", None, None),
        P("group", "shard", None),
        P("group", None, None, "shard"),
        P("group", "shard", None),
    )
    out_specs = (
        P("group", "shard", None, None),
        P("group", "shard", None),
        P("group", None, "shard", None, None),
        P("group", None, "shard", None),
    )
    return jax.shard_map(
        on_device, mesh=mesh, in_specs=in_specs, out_specs=out_specs, check_vma=False
    )
```

profile of v0, /device:TPU:72, one launch (start us, length us, event | category | flops | bytes accessed | tf_op | source)
XLA Modules:
  0.0 244.9 jit_solution(846160237460619348)
XLA Ops:
  0.6 0.7 reduce.2
  1.4 24.5 %while.28 = (s32[]{:T(128)}, f32[1536,256]{1,0:T(8,128)S(1)}, s32[1536]{0:T(1024)S(1)}, s32[4,1536]{1,0:T(4,128)}, f32[1024,256]{1,0:T(8,128)}, /*index=5*/s32[]{:T(128)}, s32[]{:T(128)}) while((s32[]{:T(128)}, f32[1536,256]{1,0:T(8,128)S(1)}, s32[1536]{0:T(1024)S(1)}, s32[4,1536]{1,0:T(4,128)}, f32[1024,256]{1,0:T(8,128)}, ...), condition=%wide.region_1.2_spmd.clone, body=%wide.region_0.0_spmd.clone.sunk | while | flops 1187843 | bytes 7906399 | solution.py:20
  1.4 0.8 fusion.17
  2.2 4.9 %gather_fusion = f32[1536,256]{1,0:T(8,128)S(1)} fusion(f32[1024,256]{1,0:T(8,128)} %get-tuple-element.319, s32[2048]{0:T(1024)S(1)} %pad_clamp_fusion.2), kind=kCustom, calls=%fused_computation.clone.clone.1 | custom fusion | bytes 3151872 | tf_op jit(solution)/shard_map/while/body/eval_jaxpr/gather | solution.py:16
  7.1 0.4 select_add_fusion.2
  7.5 0.8 fusion.17
  8.3 4.9 %gather_fusion = f32[1536,256]{1,0:T(8,128)S(1)} fusion(f32[1024,256]{1,0:T(8,128)} %get-tuple-element.319, s32[2048]{0:T(1024)S(1)} %pad_clamp_fusion.2), kind=kCustom, calls=%fused_computation.clone.clone.1 | custom fusion | bytes 3151872 | tf_op jit(solution)/shard_map/while/body/eval_jaxpr/gather | solution.py:16
  13.2 0.4 select_add_fusion.2
  13.6 0.8 fusion.17
  14.4 4.9 %gather_fusion = f32[1536,256]{1,0:T(8,128)S(1)} fusion(f32[1024,256]{1,0:T(8,128)} %get-tuple-element.319, s32[2048]{0:T(1024)S(1)} %pad_clamp_fusion.2), kind=kCustom, calls=%fused_computation.clone.clone.1 | custom fusion | bytes 3151872 | tf_op jit(solution)/shard_map/while/body/eval_jaxpr/gather | solution.py:16
  19.3 0.4 select_add_fusion.2
  19.8 0.8 fusion.17
  20.6 4.9 %gather_fusion = f32[1536,256]{1,0:T(8,128)S(1)} fusion(f32[1024,256]{1,0:T(8,128)} %get-tuple-element.319, s32[2048]{0:T(1024)S(1)} %pad_clamp_fusion.2), kind=kCustom, calls=%fused_computation.clone.clone.1 | custom fusion | bytes 3151872 | tf_op jit(solution)/shard_map/while/body/eval_jaxpr/gather | solution.py:16
  25.5 0.4 select_add_fusion.2
  25.9 0.0 copy-start.2
  25.9 1.0 convert_element_type.16
  26.9 17.3 %all-to-all-start = ((bf16[1,48,32,256]{3,2,0,1:T(8,128)(2,1)}), bf16[1,48,32,256]{3,2,0,1:T(8,128)(2,1)S(1)}, u32[]{:S(2)}, u32[]{:S(2)}) async-start(bf16[1,48,32,256]{3,2,0,1:T(8,128)(2,1)} %bitcast.4), calls=%async_computation | async-start | bytes 1572864 | tf_op jit(solution)/shard_map/all_to_all | solution.py:57
  44.1 0.0 copy-done.2
  44.2 0.8 copy.20
  45.0 0.1 bitcast_add_fusion
  45.1 30.0 %all-to-all-done = bf16[1,48,32,256]{3,2,0,1:T(8,128)(2,1)S(1)} async-done(((bf16[1,48,32,256]{3,2,0,1:T(8,128)(2,1)}), bf16[1,48,32,256]{3,2,0,1:T(8,128)(2,1)S(1)}, u32[]{:S(2)}, u32[]{:S(2)}) %all-to-all-start) | async-done | bytes 786464 | tf_op jit(solution)/shard_map/all_to_all | solution.py:57
  75.2 1.6 fusion.6
  76.8 0.0 copy-start.4
  76.8 1.1 copy.22
  77.9 8.1 %all-to-all-start.1 = ((bf16[48,1,32,256]{3,2,1,0:T(8,128)(2,1)}), bf16[48,1,32,256]{3,2,1,0:T(8,128)(2,1)S(1)}, u32[]{:S(2)}, u32[]{:S(2)}) async-start(bf16[48,1,32,256]{3,2,1,0:T(8,128)(2,1)} %copy.22), calls=%async_computation.1 | async-start | bytes 1572864 | tf_op jit(solution)/shard_map/all_to_all | solution.py:69
  86.0 0.0 copy-done.4
  86.0 0.1 copy.24
  86.1 0.1 reduce.3
  86.3 0.1 compare_select_fusion.3
  86.4 0.1 reshape.284
  86.4 0.1 iota_compare_fusion
  86.5 29.1 %all-to-all-done.1 = bf16[48,1,32,256]{3,2,1,0:T(8,128)(2,1)S(1)} async-done(((bf16[48,1,32,256]{3,2,1,0:T(8,128)(2,1)}), bf16[48,1,32,256]{3,2,1,0:T(8,128)(2,1)S(1)}, u32[]{:S(2)}, u32[]{:S(2)}) %all-to-all-start.1) | async-done | bytes 786464 | tf_op jit(solution)/shard_map/all_to_all | solution.py:69
  115.6 0.2 bitcast_convert_fusion
  115.7 0.1 broadcast_in_dim.93
  115.8 0.0 copy-start.3
  115.8 43.5 %while.27 = (s32[]{:T(128)}, f32[1024,256]{1,0:T(8,128)S(1)}, s32[4,1536]{1,0:T(4,128)}, s32[1536]{0:T(1024)S(1)}, f32[1536,256]{1,0:T(8,128)S(1)}, /*index=5*/s32[]{:T(128)}, f32[]{:T(128)}) while((s32[]{:T(128)}, f32[1024,256]{1,0:T(8,128)S(1)}, s32[4,1536]{1,0:T(4,128)}, s32[1536]{0:T(1024)S(1)}, f32[1536,256]{1,0:T(8,128)S(1)}, ...), condition=%wide.region_4.5_spmd, body=%wide.region_2.4_spmd.sunk | while | flops 792578 | bytes 2643545 | solution.py:31
  115.8 0.8 fusion.16
  116.6 10.1 %scatter_custom_fusion.5 = f32[1024,256]{1,0:T(8,128)S(1)} fusion(f32[1024,256]{1,0:T(8,128)S(1)} %get-tuple-element.330, s32[1536]{0:T(1024)S(1)} %fusion.16, f32[1536,256]{1,0:T(8,128)S(1)} %get-tuple-element.340, f32[]{:T(128)} %constant.85.clone.1..sunk, pred[1536]{0:T(1024)(128)(4,1)S(1)} %broadcast_compare_fusion.4), kind=kCustom, calls=%fused_computation.4.clone.1 | custom fusion | flops 786432 | bytes 2623492 | tf_op jit(solution)/shard_map/while/body/eval_jaxpr/scatter-add | solution.py:28
  126.7 0.8 fusion.16
  127.5 10.1 %scatter_custom_fusion.5 = f32[1024,256]{1,0:T(8,128)S(1)} fusion(f32[1024,256]{1,0:T(8,128)S(1)} %get-tuple-element.330, s32[1536]{0:T(1024)S(1)} %fusion.16, f32[1536,256]{1,0:T(8,128)S(1)} %get-tuple-element.340, f32[]{:T(128)} %constant.85.clone.1..sunk, pred[1536]{0:T(1024)(128)(4,1)S(1)} %broadcast_compare_fusion.4), kind=kCustom, calls=%fused_computation.4.clone.1 | custom fusion | flops 786432 | bytes 2623492 | tf_op jit(solution)/shard_map/while/body/eval_jaxpr/scatter-add | solution.py:28
  137.6 0.8 fusion.16
  138.4 10.1 %scatter_custom_fusion.5 = f32[1024,256]{1,0:T(8,128)S(1)} fusion(f32[1024,256]{1,0:T(8,128)S(1)} %get-tuple-element.330, s32[1536]{0:T(1024)S(1)} %fusion.16, f32[1536,256]{1,0:T(8,128)S(1)} %get-tuple-element.340, f32[]{:T(128)} %constant.85.clone.1..sunk, pred[1536]{0:T(1024)(128)(4,1)S(1)} %broadcast_compare_fusion.4), kind=kCustom, calls=%fused_computation.4.clone.1 | custom fusion | flops 786432 | bytes 2623492 | tf_op jit(solution)/shard_map/while/body/eval_jaxpr/scatter-add | solution.py:28
  148.5 0.8 fusion.16
  149.3 10.1 %scatter_custom_fusion.5 = f32[1024,256]{1,0:T(8,128)S(1)} fusion(f32[1024,256]{1,0:T(8,128)S(1)} %get-tuple-element.330, s32[1536]{0:T(1024)S(1)} %fusion.16, f32[1536,256]{1,0:T(8,128)S(1)} %get-tuple-element.340, f32[]{:T(128)} %constant.85.clone.1..sunk, pred[1536]{0:T(1024)(128)(4,1)S(1)} %broadcast_compare_fusion.4), kind=kCustom, calls=%fused_computation.4.clone.1 | custom fusion | flops 786432 | bytes 2623492 | tf_op jit(solution)/shard_map/while/body/eval_jaxpr/scatter-add | solution.py:28
  159.3 0.0 copy-start
  159.3 0.2 multiply_reduce_fusion
  159.6 0.0 copy-done.3
  159.6 1.0 copy-done
  160.6 0.2 divide_subtract_fusion
  160.8 0.0 copy-start.1
  160.8 3.5 %gather_fusion.1 = f32[1024,256]{1,0:T(8,128)S(1)} fusion(f32[1024,256]{1,0:T(8,128)S(1)} %divide_subtract_fusion, s32[1024]{0:T(1024)S(1)} %broadcast_clamp_fusion), kind=kCustom, calls=%fused_computation.1 | custom fusion | bytes 2101248 | tf_op jit(solution)/shard_map/gather | solution.py:80
  164.3 0.0 copy-done.1
  164.3 4.5 %gather_fusion.2 = f32[1024]{0:T(1024)S(1)} fusion(f32[1024]{0:T(1024)S(1)} %get-tuple-element.237, s32[1024]{0:T(1024)S(1)} %broadcast_clamp_fusion), kind=kCustom, calls=%fused_computation.2 | custom fusion | bytes 12288 | tf_op jit(solution)/shard_map/gather | solution.py:81
  168.8 0.1 gather.17
  168.9 0.7 compare_select_fusion.2
  169.6 12.5 %all-to-all-start.3 = ((f32[16,1,64]{2,1,0:T(1,128)}), f32[16,1,64]{2,1,0:T(1,128)S(1)}, u32[]{:S(2)}, u32[]{:S(2)}) async-start(f32[16,1,64]{2,1,0:T(1,128)} %compare_select_fusion.2), calls=%async_computation.3 | async-start | bytes 16384 | tf_op jit(solution)/shard_map/all_to_all | solution.py:84
  182.1 1.2 broadcast_select_fusion
  183.2 11.1 %all-to-all-done.3 = f32[16,1,64]{2,1,0:T(1,128)S(1)} async-done(((f32[16,1,64]{2,1,0:T(1,128)}), f32[16,1,64]{2,1,0:T(1,128)S(1)}, u32[]{:S(2)}, u32[]{:S(2)}) %all-to-all-start.3) | async-done | bytes 4128 | tf_op jit(solution)/shard_map/all_to_all | solution.py:84
  194.4 3.7 %all-to-all-start.2 = ((f32[16,64,256]{2,1,0:T(8,128)}), f32[16,64,256]{2,1,0:T(8,128)S(1)}, u32[]{:S(2)}, u32[]{:S(2)}) async-start(f32[16,64,256]{2,1,0:T(8,128)} %broadcast_select_fusion), calls=%async_computation.2 | async-start | bytes 2097152 | tf_op jit(solution)/shard_map/all_to_all | solution.py:83
  198.0 0.6 add.136
  198.6 44.7 %all-to-all-done.2 = f32[16,64,256]{2,1,0:T(8,128)S(1)} async-done(((f32[16,64,256]{2,1,0:T(8,128)}), f32[16,64,256]{2,1,0:T(8,128)S(1)}, u32[]{:S(2)}, u32[]{:S(2)}) %all-to-all-start.2) | async-done | bytes 1048608 | tf_op jit(solution)/shard_map/all_to_all | solution.py:83
  243.3 1.0 copy.48
  244.3 0.6 copy.49
  (17 shorter events, 0.1 us)
Async XLA Ops:
  25.9 18.2 %copy-start.2 = (f32[1,48,48,32]{2,3,1,0:T(8,128)S(1)}, f32[1,48,48,32]{2,3,1,0:T(8,128)}, u32[]{:S(2)}) copy-start(f32[1,48,48,32]{2,3,1,0:T(8,128)} %param.14) | copy-start | bytes 884740
  26.9 48.3 %all-to-all-start = ((bf16[1,48,32,256]{3,2,0,1:T(8,128)(2,1)}), bf16[1,48,32,256]{3,2,0,1:T(8,128)(2,1)S(1)}, u32[]{:S(2)}, u32[]{:S(2)}) async-start(bf16[1,48,32,256]{3,2,0,1:T(8,128)(2,1)} %bitcast.4), calls=%async_computation | async-start | bytes 1572864 | tf_op jit(solution)/shard_map/all_to_all | solution.py:57
  76.8 9.3 %copy-start.4 = (s32[1,1,16]{2,1,0:T(1,128)S(1)}, s32[1,1,16]{2,1,0:T(1,128)}, u32[]{:S(2)}) copy-start(s32[1,1,16]{2,1,0:T(1,128)} %param.15) | copy-start | bytes 196
  77.9 37.7 %all-to-all-start.1 = ((bf16[48,1,32,256]{3,2,1,0:T(8,128)(2,1)}), bf16[48,1,32,256]{3,2,1,0:T(8,128)(2,1)S(1)}, u32[]{:S(2)}, u32[]{:S(2)}) async-start(bf16[48,1,32,256]{3,2,1,0:T(8,128)(2,1)} %copy.22), calls=%async_computation.1 | async-start | bytes 1572864 | tf_op jit(solution)/shard_map/all_to_all | solution.py:69
  115.8 43.7 %copy-start.3 = (f32[1,1,1024]{2,1,0:T(1,128)S(1)}, f32[1,1,1024]{2,1,0:T(1,128)}, u32[]{:S(2)}) copy-start(f32[1,1,1024]{2,1,0:T(1,128)} %param.11) | copy-start | bytes 12292
  159.3 1.2 copy-start
  160.8 3.5 %copy-start.1 = (f32[1024,256]{1,0:T(8,128)}, f32[1024,256]{1,0:T(8,128)S(1)}, u32[]{:S(2)}) copy-start(f32[1024,256]{1,0:T(8,128)S(1)} %divide_subtract_fusion) | copy-start | bytes 3145732
  169.6 24.8 %all-to-all-start.3 = ((f32[16,1,64]{2,1,0:T(1,128)}), f32[16,1,64]{2,1,0:T(1,128)S(1)}, u32[]{:S(2)}, u32[]{:S(2)}) async-start(f32[16,1,64]{2,1,0:T(1,128)} %compare_select_fusion.2), calls=%async_computation.3 | async-start | bytes 16384 | tf_op jit(solution)/shard_map/all_to_all | solution.py:84
  194.4 49.0 %all-to-all-start.2 = ((f32[16,64,256]{2,1,0:T(8,128)}), f32[16,64,256]{2,1,0:T(8,128)S(1)}, u32[]{:S(2)}, u32[]{:S(2)}) async-start(f32[16,64,256]{2,1,0:T(8,128)} %broadcast_select_fusion), calls=%async_computation.2 | async-start | bytes 2097152 | tf_op jit(solution)/shard_map/all_to_all | solution.py:83
where the time goes:
time: 246 us; the launch traced here: 245 us
  waiting for transfers between devices  115 us (47%)
  other arithmetic  53.4 us (22%)
  starting transfers between devices  41.5 us (17%)
  local copies, waits for them, and re-layouts  32.4 us (13%)
    all_to_all x1, waiting for transfers between devices, on_device(): lax.all_to_all(moved_rows, 'group', split_axis=0, concat_axis=0, tiled=True)  44.7 us
    scatter-add x4, other arithmetic, row_add_slot(): return running.at[bag_rows[bag_slot]].add(masked)  40.3 us
    all_to_all x1, waiting for transfers between devices, on_device(): lax.all_to_all(pooled.reshape(1, shards, per_shard, row_width), 'shard',...  30 us
    all_to_all x1, waiting for transfers between devices, on_device(): lax.all_to_all(upstream.reshape(shards, 1, per_shard, row_width), 'shard'...  29.1 us
    gather x4, local copies, waits for them, and re-layouts, pool_add_slot(): picked = rows_table[bag_rows[bag_slot]]  19.6 us
    all_to_all x1, starting transfers between devices, on_device(): lax.all_to_all(pooled.reshape(1, shards, per_shard, row_width), 'shard',...  17.3 us
    all_to_all x1, starting transfers between devices, on_device(): lax.all_to_all(moved_state, 'group', split_axis=0, concat_axis=0, tiled=T...  12.5 us
    all_to_all x1, waiting for transfers between devices, on_device(): lax.all_to_all(moved_state, 'group', split_axis=0, concat_axis=0, tiled=T...  11.1 us
  transfers between devices with their start and end apart: 4, of which 4 were waited for; matrix products, arithmetic and copies ran while one was open for 1% of the time, Pallas kernels for 0%

commit v1 on v0

v1 whole, which is shorter than its diff:
```python
import jax
import jax.numpy as jnp
from jax import lax
from jax.sharding import PartitionSpec as P

CAP = 64


learn_rate = 0.05
epsilon = 1e-08


def three_parts(values):
    high = lax.reduce_precision(values, 8, 7)
    rest = values - high
    middle = lax.reduce_precision(rest, 8, 7)
    low = rest - middle
    return [part.astype(jnp.bfloat16) for part in (high, middle, low)]


def hits(live_ids, num_rows):
    rows = jnp.arange(num_rows, dtype=jnp.int32)
    total = 0.0
    for slot in range(live_ids.shape[0]):
        total = total + jnp.where(live_ids[slot][:, None] == rows[None, :], 1.0, 0.0)
    return total.astype(jnp.bfloat16)


def on_device(table, row_state, bag_ids, bag_lengths, interaction_grad, move_rows):
    rows_table = table[0, 0]
    state_rows = row_state[0, 0]
    bag_rows = bag_ids[0, 0]
    bag_len = bag_lengths[0, 0]
    counts = move_rows[0, 0]
    grad_block = interaction_grad[0]
    shards = lax.axis_size("shard")
    groups = lax.axis_size("group")
    samples = bag_rows.shape[1]
    per_shard = samples // shards
    row_width = rows_table.shape[1]
    num_rows = rows_table.shape[0]
    slots = jnp.arange(bag_rows.shape[0], dtype=jnp.int32)[:, None]
    live_ids = jnp.where(slots < bag_len[None, :], bag_rows, -1)
    hit = hits(live_ids, num_rows)
    pooled = sum(
        jnp.dot(hit, part, preferred_element_type=jnp.float32) for part in three_parts(rows_table)
    ).astype(jnp.bfloat16)
    received = lax.all_to_all(
        pooled.reshape(1, shards, per_shard, row_width),
        "shard",
        split_axis=1,
        concat_axis=0,
        tiled=True,
    )
    received = received.reshape(shards, per_shard, row_width)
    symmetric = grad_block + jnp.transpose(grad_block, (1, 0, 2))
    upstream = jnp.einsum(
        "fgb,gbe->fbe", symmetric, received.astype(jnp.float32), precision=lax.Precision.HIGHEST
    ).astype(jnp.bfloat16)
    returned = lax.all_to_all(
        upstream.reshape(shards, 1, per_shard, row_width),
        "shard",
        split_axis=0,
        concat_axis=1,
        tiled=True,
    )
    returned = returned.reshape(samples, row_width)
    row_grads = lax.dot_general(
        hit, returned, (((0,), (0,)), ((), ())), preferred_element_type=jnp.float32
    )
    new_state = state_rows + jnp.mean(row_grads * row_grads, axis=-1)
    new_rows = rows_table - learn_rate * row_grads / (jnp.sqrt(new_state)[:, None] + epsilon)
    starts = jnp.cumsum(counts) - counts
    offsets = jnp.arange(CAP, dtype=jnp.int32)
    live_slots = offsets[None, :] < counts[:, None]
    scale = jnp.maximum(jnp.max(jnp.abs(new_rows), axis=-1), 1e-30)
    coded = jnp.round(new_rows * (32767.0 / scale)[:, None])
    tail = jnp.zeros((CAP, row_width), jnp.float32)
    padded = jnp.concatenate([coded, tail], axis=0)
    side = jnp.stack([new_state, scale * (1.0 / 32767.0)], axis=0)
    side = jnp.concatenate([side, jnp.zeros((2, CAP), jnp.float32)], axis=1)
    blocks = []
    sides = []
    for group in range(groups):
        block = lax.dynamic_slice_in_dim(padded, starts[group], CAP, axis=0)
        blocks.append(jnp.where(live_slots[group][:, None], block, 0.0).astype(jnp.int16))
        both = lax.dynamic_slice_in_dim(side, starts[group], CAP, axis=1)
        sides.append(jnp.where(live_slots[group][None, :], both, 0.0))
    arrived_code, arrived_side = (
        lax.all_to_all(jnp.stack(blocks), "group", split_axis=0, concat_axis=0, tiled=True),
        lax.all_to_all(jnp.stack(sides), "group", split_axis=0, concat_axis=0, tiled=True),
    )
    arrived = arrived_code.astype(jnp.float32) * arrived_side[:, 1, :, None]
    return (
        new_rows[None, None],
        new_state[None, None],
        arrived.reshape(1, groups, 1, CAP, row_width),
        arrived_side[:, 0].reshape(1, groups, 1, CAP),
    )


def solution(mesh):
    in_specs = (
        P("group", "shard", None, None),
        P("group", "shard", None),
        P("group", "shard", None, None),
        P("group", "shard", None),
        P("group", None, None, "shard"),
        P("group", "shard", None),
    )
    out_specs = (
        P("group", "shard", None, None),
        P("group", "shard", None),
        P("group", None, "shard", None, None),
        P("group", None, "shard", None),
    )
    return jax.shard_map(
        on_device, mesh=mesh, in_specs=in_specs, out_specs=out_specs, check_vma=False
    )
```

time: 246 us -> 179 us (0.73)
  the two profiles are of different devices: /device:TPU:72 before, /device:TPU:15 now
where the time goes in v1:
time: 179 us; the launch traced here: 178 us
  waiting for transfers between devices  58.4 us (33%)
  starting transfers between devices  48.8 us (27%)
  between operations  31 us (17%)
  matrix products  17.6 us (10%)
  other arithmetic  17.4 us (10%)
  local copies, waits for them, and re-layouts  4.76 us (3%)
    all_to_all x1, waiting for transfers between devices, on_device(): lax.all_to_all(pooled.reshape(1, shards, per_shard, row_width), 'shard',...  26 us
    all_to_all x1, waiting for transfers between devices, on_device(): lax.all_to_all(jnp.stack(blocks), 'group', split_axis=0, concat_axis=0, t...  23 us
    all_to_all x1, starting transfers between devices, on_device(): lax.all_to_all(pooled.reshape(1, shards, per_shard, row_width), 'shard',...  17.7 us
    all_to_all x1, starting transfers between devices, on_device(): lax.all_to_all(jnp.stack(sides), 'group', split_axis=0, concat_axis=0, ti...  14.8 us
    unnamed x32, other arithmetic  13.6 us
    dot_general x3, matrix products, on_device(): jnp.dot(hit, part, preferred_element_type=jnp.float32)  12.4 us
    all_to_all x1, starting transfers between devices, on_device(): lax.all_to_all(upstream.reshape(shards, 1, per_shard, row_width), 'shard'...  10.5 us
    all_to_all x1, waiting for transfers between devices, on_device(): lax.all_to_all(jnp.stack(sides), 'group', split_axis=0, concat_axis=0, ti...  9.33 us
  transfers between devices with their start and end apart: 4, of which 3 were waited for; matrix products, arithmetic and copies ran while one was open for 3% of the time, Pallas kernels for 0%

profile of v1, /device:TPU:15, one launch (start us, length us, event | category | flops | bytes accessed | tf_op | source)
XLA Modules:
  0.0 178.0 jit_solution(9021314595611388018)
XLA Ops:
  0.6 0.7 reduce
  1.3 0.7 bitcast_select_fusion
  2.1 0.1 slice_reduce_fusion.3
  2.2 4.7 %fusion.2 = f32[1536,256]{1,0:T(8,128)S(1)} fusion(s32[1536]{0:T(1024)S(1)} %get-tuple-element.17, s32[1536]{0:T(1024)S(1)} %get-tuple-element.18, s32[1536]{0:T(1024)S(1)} %get-tuple-element.19, s32[1536]{0:T(1024)S(1)} %get-tuple-element.16, f32[1,1,1024,256]{3,2,1,0:T(8,128)} %param.6), kind=kOutput, calls=%fused_computation.9 | convolution fusion | flops 824705024 | bytes 2646016 | tf_op jit(solution)/shard_map/dot_general | solution.py:46
  6.9 3.4 %convolution_add_fusion.1 = f32[1536,256]{1,0:T(8,128)S(1)} fusion(f32[1536,256]{1,0:T(8,128)S(1)} %fusion.2, s32[1536]{0:T(1024)S(1)} %get-tuple-element.17, s32[1536]{0:T(1024)S(1)} %get-tuple-element.18, s32[1536]{0:T(1024)S(1)} %get-tuple-element.19, s32[1536]{0:T(1024)S(1)} %get-tuple-element.16, f32[1,1,1024,256]{3,2,1,0:T(8,128)S(1)} %copy-done.2), kind=kOutput, calls=%fused_computation.6 | convolution fusion | flops 825622528 | bytes 4218880 | tf_op jit(solution)/shard_map/dot_general | solution.py:46
  10.3 4.3 %fusion = bf16[1536,256]{1,0:T(8,128)(2,1)} fusion(f32[1536,256]{1,0:T(8,128)S(1)} %convolution_add_fusion.1, s32[1536]{0:T(1024)S(1)} %get-tuple-element.17, s32[1536]{0:T(1024)S(1)} %get-tuple-element.18, s32[1536]{0:T(1024)S(1)} %get-tuple-element.19, s32[1536]{0:T(1024)S(1)} %get-tuple-element.16, f32[1,1,1024,256]{3,2,1,0:T(8,128)S(1)} %copy-done.2), kind=kOutput, calls=%fused_computation.7 | convolution fusion | flops 826277888 | bytes 3432448 | tf_op jit(solution)/shard_map/dot_general | solution.py:46
  14.6 17.7 %all-to-all-start = ((bf16[1,48,32,256]{3,2,0,1:T(8,128)(2,1)}), bf16[1,48,32,256]{3,2,0,1:T(8,128)(2,1)S(1)}, u32[]{:S(2)}, u32[]{:S(2)}) async-start(bf16[1,48,32,256]{3,2,0,1:T(8,128)(2,1)} %bitcast.3), calls=%async_computation | async-start | bytes 1572864 | tf_op jit(solution)/shard_map/all_to_all | solution.py:48
  32.4 0.8 copy.25
  33.2 0.1 bitcast_add_fusion
  33.3 26.0 %all-to-all-done = bf16[1,48,32,256]{3,2,0,1:T(8,128)(2,1)S(1)} async-done(((bf16[1,48,32,256]{3,2,0,1:T(8,128)(2,1)}), bf16[1,48,32,256]{3,2,0,1:T(8,128)(2,1)S(1)}, u32[]{:S(2)}, u32[]{:S(2)}) %all-to-all-start) | async-done | bytes 786464 | tf_op jit(solution)/shard_map/all_to_all | solution.py:48
  59.4 1.6 fusion.3
  61.0 1.1 copy.27
  62.1 10.5 %all-to-all-start.1 = ((bf16[48,1,32,256]{3,2,1,0:T(8,128)(2,1)}), bf16[48,1,32,256]{3,2,1,0:T(8,128)(2,1)S(1)}, u32[]{:S(2)}, u32[]{:S(2)}) async-start(bf16[48,1,32,256]{3,2,1,0:T(8,128)(2,1)} %copy.27), calls=%async_computation.1 | async-start | bytes 1572864 | tf_op jit(solution)/shard_map/all_to_all | solution.py:60
  72.6 0.1 copy.28
  72.8 0.1 reduce.5
  72.9 0.7 fusion.49
  103.8 0.1 iota_compare_fusion.5
  103.9 0.0 copy-start.3
  103.9 3.6 %multiply_reduce_fusion = (f32[1024]{0:T(1024)S(1)}, f32[1024,256]{1,0:T(8,128)S(1)}) fusion(bf16[1536,256]{1,0:T(8,128)(2,1)S(1)} %bitcast.195, s32[1536]{0:T(1024)S(1)} %get-tuple-element.17, s32[1536]{0:T(1024)S(1)} %get-tuple-element.18, s32[1536]{0:T(1024)S(1)} %get-tuple-element.19, s32[1536]{0:T(1024)S(1)} %get-tuple-element.16), kind=kOutput, calls=%fused_computation.21 | convolution fusion | flops 824704000 | bytes 1863680 | tf_op jit(solution)/shard_map/dot_general | solution.py:68
  107.6 0.4 abs_reduce_fusion
  108.0 0.2 multiply_round-nearest-even_fusion
  108.3 0.7 constant_dynamic-update-slice_fusion.15
  109.0 0.1 constant_dynamic-update-slice_fusion.31
  109.1 0.7 constant_dynamic-update-slice_fusion.14
  109.8 0.1 constant_dynamic-update-slice_fusion.30
  109.8 0.7 constant_dynamic-update-slice_fusion.13
  110.5 0.1 constant_dynamic-update-slice_fusion.29
  110.6 0.7 constant_dynamic-update-slice_fusion.12
  111.3 0.1 constant_dynamic-update-slice_fusion.28
  111.4 0.7 constant_dynamic-update-slice_fusion.11
  112.1 0.1 constant_dynamic-update-slice_fusion.27
  112.2 0.7 constant_dynamic-update-slice_fusion.10
  112.9 0.1 constant_dynamic-update-slice_fusion.26
  113.0 0.7 constant_dynamic-update-slice_fusion.9
  113.7 0.1 constant_dynamic-update-slice_fusion.25
  113.7 0.7 constant_dynamic-update-slice_fusion.8
  114.4 0.1 constant_dynamic-update-slice_fusion.24
  114.5 0.7 constant_dynamic-update-slice_fusion.7
  115.2 0.1 constant_dynamic-update-slice_fusion.23
  115.3 0.7 constant_dynamic-update-slice_fusion.6
  116.0 0.1 constant_dynamic-update-slice_fusion.22
  116.1 0.7 constant_dynamic-update-slice_fusion.5
  116.8 0.1 constant_dynamic-update-slice_fusion.21
  116.9 0.7 constant_dynamic-update-slice_fusion.4
  117.6 0.1 constant_dynamic-update-slice_fusion.20
  117.6 0.7 constant_dynamic-update-slice_fusion.3
  118.3 0.1 constant_dynamic-update-slice_fusion.19
  118.4 0.7 constant_dynamic-update-slice_fusion.2
  119.1 0.1 constant_dynamic-update-slice_fusion.18
  119.2 0.7 constant_dynamic-update-slice_fusion.1
  119.9 0.1 constant_dynamic-update-slice_fusion.17
  120.0 0.1 constant_dynamic-update-slice_fusion.16
  120.1 0.7 reshape.151
  120.8 14.8 %all-to-all-start.3 = ((f32[16,1,128]{2,1,0:T(1,128)}), f32[16,1,128]{2,1,0:T(1,128)S(1)}, u32[]{:S(2)}, u32[]{:S(2)}) async-start(f32[16,1,128]{2,1,0:T(1,128)} %reshape.151), calls=%async_computation.3 | async-start | bytes 16384 | tf_op jit(solution)/shard_map/all_to_all | solution.py:91
  135.6 0.7 constant_dynamic-update-slice_fusion
  136.3 9.3 %all-to-all-done.3 = f32[16,1,128]{2,1,0:T(1,128)S(1)} async-done(((f32[16,1,128]{2,1,0:T(1,128)}), f32[16,1,128]{2,1,0:T(1,128)S(1)}, u32[]{:S(2)}, u32[]{:S(2)}) %all-to-all-start.3) | async-done | bytes 8224 | tf_op jit(solution)/shard_map/all_to_all | solution.py:91
  145.6 5.8 %all-to-all-start.2 = ((s16[16,64,256]{2,1,0:T(8,128)(2,1)}), s16[16,64,256]{2,1,0:T(8,128)(2,1)S(1)}, u32[]{:S(2)}, u32[]{:S(2)}) async-start(s16[16,64,256]{2,1,0:T(8,128)(2,1)} %constant_dynamic-update-slice_fusion), calls=%async_computation.2 | async-start | bytes 1048576 | tf_op jit(solution)/shard_map/all_to_all | solution.py:90
  151.3 0.6 add.125
  151.9 0.5 broadcast.70
  152.5 0.7 reduce.10
  153.1 0.1 reshape.152
  153.2 0.6 slice_bitcast_fusion
  153.8 23.0 %all-to-all-done.2 = s16[16,64,256]{2,1,0:T(8,128)(2,1)S(1)} async-done(((s16[16,64,256]{2,1,0:T(8,128)(2,1)}), s16[16,64,256]{2,1,0:T(8,128)(2,1)S(1)}, u32[]{:S(2)}, u32[]{:S(2)}) %all-to-all-start.2) | async-done | bytes 524320 | tf_op jit(solution)/shard_map/all_to_all | solution.py:90
  176.9 1.2 multiply_bitcast_fusion
  (19 shorter events, 0.1 us)
Async XLA Ops:
  2.2 4.7 %copy-start.2 = (f32[1,1,1024,256]{3,2,1,0:T(8,128)S(1)}, f32[1,1,1024,256]{3,2,1,0:T(8,128)}, u32[]{:S(2)}) copy-start(f32[1,1,1024,256]{3,2,1,0:T(8,128)} %param.6) | copy-start | bytes 3145732
  14.6 17.8 %copy-start.1 = (f32[1,48,48,32]{2,3,1,0:T(8,128)S(1)}, f32[1,48,48,32]{2,3,1,0:T(8,128)}, u32[]{:S(2)}) copy-start(f32[1,48,48,32]{2,3,1,0:T(8,128)} %param.10) | copy-start | bytes 884740
  14.6 44.8 %all-to-all-start = ((bf16[1,48,32,256]{3,2,0,1:T(8,128)(2,1)}), bf16[1,48,32,256]{3,2,0,1:T(8,128)(2,1)S(1)}, u32[]{:S(2)}, u32[]{:S(2)}) async-start(bf16[1,48,32,256]{3,2,0,1:T(8,128)(2,1)} %bitcast.3), calls=%async_computation | async-start | bytes 1572864 | tf_op jit(solution)/shard_map/all_to_all | solution.py:48
  61.0 11.7 %copy-start.5 = (s32[1,1,16]{2,1,0:T(1,128)S(1)}, s32[1,1,16]{2,1,0:T(1,128)}, u32[]{:S(2)}) copy-start(s32[1,1,16]{2,1,0:T(1,128)} %param.11) | copy-start | bytes 196
  62.1 41.8 %all-to-all-start.1 = ((bf16[48,1,32,256]{3,2,1,0:T(8,128)(2,1)}), bf16[48,1,32,256]{3,2,1,0:T(8,128)(2,1)S(1)}, u32[]{:S(2)}, u32[]{:S(2)}) async-start(bf16[48,1,32,256]{3,2,1,0:T(8,128)(2,1)} %copy.27), calls=%async_computation.1 | async-start | bytes 1572864 | tf_op jit(solution)/shard_map/all_to_all | solution.py:60
  103.9 3.6 %copy-start.4 = (f32[1,1,1024]{2,1,0:T(1,128)S(1)}, f32[1,1,1024]{2,1,0:T(1,128)}, u32[]{:S(2)}) copy-start(f32[1,1,1024]{2,1,0:T(1,128)} %param.7) | copy-start | bytes 12292
  103.9 3.7 %copy-start.3 = (f32[1,1,1024,256]{3,2,1,0:T(8,128)S(1)}, f32[1,1,1024,256]{3,2,1,0:T(8,128)}, u32[]{:S(2)}) copy-start(f32[1,1,1024,256]{3,2,1,0:T(8,128)} %param.6) | copy-start | bytes 3145732
  108.0 1.0 copy-start
  120.8 24.8 %all-to-all-start.3 = ((f32[16,1,128]{2,1,0:T(1,128)}), f32[16,1,128]{2,1,0:T(1,128)S(1)}, u32[]{:S(2)}, u32[]{:S(2)}) async-start(f32[16,1,128]{2,1,0:T(1,128)} %reshape.151), calls=%async_computation.3 | async-start | bytes 16384 | tf_op jit(solution)/shard_map/all_to_all | solution.py:91
  145.6 31.3 %all-to-all-start.2 = ((s16[16,64,256]{2,1,0:T(8,128)(2,1)}), s16[16,64,256]{2,1,0:T(8,128)(2,1)S(1)}, u32[]{:S(2)}, u32[]{:S(2)}) async-start(s16[16,64,256]{2,1,0:T(8,128)(2,1)} %constant_dynamic-update-slice_fusion), calls=%async_computation.2 | async-start | bytes 1048576 | tf_op jit(solution)/shard_map/all_to_all | solution.py:90

commit v2 on v0

v2 whole, which is shorter than its diff:
```python
import functools

import jax
import jax.numpy as jnp
from jax import lax
from jax.experimental import pallas as pl
from jax.experimental.pallas import tpu as pltpu
from jax.sharding import PartitionSpec as P

MESH = pl.DeviceIdType.MESH
CAP = 64
PARTS = 2
TOP = 32767.0

learn_rate = 0.05
epsilon = 1e-08


def split_three(values):
    high = values.astype(jnp.bfloat16)
    rest = values - high.astype(jnp.float32)
    middle = rest.astype(jnp.bfloat16)
    low = (rest - middle.astype(jnp.float32)).astype(jnp.bfloat16)
    return high, middle, low


def bag_kernel(
    groups, shards, line,
    table_ref, state_ref, ids_ref, len_ref, grad_ref, counts_ref,
    new_table_ref, new_state_ref, code_ref, side_ref,
    ids_col, ids_row, parts, hit, mix, send1, recv1, send2, recv2,
    in_left, in_right, out_left, out_right, grads, state_col, coded, side_col, pick,
    code_send, code_recv, side_send, side_recv, starts,
    send1_sem, recv1_sem, send2_sem, recv2_sem, code_sem, side_sem,
):
    rows, width = table_ref.shape
    slots, samples = ids_ref.shape
    deep = samples // shards // PARTS
    half = width // 2
    part_rows = shards * deep
    lines = shards // line
    group = lax.axis_index("group")
    me = lax.axis_index("shard")
    my_line = me // line
    my_spot = me % line

    wing = groups // 2
    my_wing = group // wing
    my_place = group % wing

    def dest(k):
        return ((my_wing + 1 + k // wing) % 2) * wing + (my_place + k) % wing

    barrier = pltpu.get_barrier_semaphore()

    def greet_shard(k, carry):
        pl.semaphore_signal(
            barrier, inc=1, device_id=(group, (me + k) % shards), device_id_type=MESH
        )
        return carry

    def greet_group(k, carry):
        pl.semaphore_signal(
            barrier, inc=1, device_id=((group + k) % groups, me), device_id_type=MESH
        )
        return carry

    lax.fori_loop(1, shards, greet_shard, 0)
    lax.fori_loop(1, groups, greet_group, 0)

    def block_copy(source, target, send_sem, recv_sem, part, other):
        return pltpu.make_async_remote_copy(
            src_ref=source.at[part, other],
            dst_ref=target.at[part, me],
            send_sem=send_sem.at[part],
            recv_sem=recv_sem.at[part],
            device_id=(group, other),
            device_id_type=MESH,
        )

    def all_blocks(source, target, send_sem, recv_sem, part):
        return pltpu.make_async_remote_copy(
            src_ref=source.at[part, pl.ds(0, shards - 1)],
            dst_ref=target.at[part, pl.ds(0, shards - 1)],
            send_sem=send_sem.at[part],
            recv_sem=recv_sem.at[part],
            device_id=(group, (me + 1) % shards),
            device_id_type=MESH,
        )

    def send_line(source, target, send_sem, recv_sem, part, step):
        first = ((my_line + step) % lines) * line
        for turn in range(line):
            other = first + (my_spot + turn) % line
            copy = block_copy(source, target, send_sem, recv_sem, part, other)
            if turn == 0:
                pl.when(step > 0)(copy.start)
            else:
                copy.start()

    slot = lax.broadcasted_iota(jnp.int32, (slots, samples), 0)
    live = jnp.where(slot < len_ref[...], ids_ref[...], -1)
    live = jnp.concatenate([live, jnp.full((8 - slots, samples), -1, jnp.int32)], axis=0)
    columns = live.T.reshape(shards, PARTS, deep, 8)
    for part in range(PARTS):
        ids_col[part] = columns[:, part]

    high, middle, low = split_three(table_ref[...])
    parts[:, 0:width] = high
    parts[:, width:2 * width] = middle
    parts[:, 2 * width:3 * width] = low

    pl.semaphore_wait(barrier, shards + groups - 2)

    for part in range(PARTS):
        def pool_step(step, carry, part=part):
            first = ((my_line + step) % lines) * line
            column = ids_col[part, pl.ds(first, line)].reshape(line * deep, 8)
            lane = lax.broadcasted_iota(jnp.int32, (line * deep, rows), 1)
            total = jnp.zeros((line * deep, rows), jnp.float32)
            for j in range(slots):
                total = total + jnp.where(column[:, j:j + 1] == lane, 1.0, 0.0)
            product = jnp.dot(
                total.astype(jnp.bfloat16), parts[...], preferred_element_type=jnp.float32
            )
            pooled = product[:, 0:width] + product[:, width:2 * width]
            pooled = pooled + product[:, 2 * width:3 * width]
            send1[part, pl.ds(first, line)] = pooled.astype(jnp.bfloat16).reshape(line, deep, width)
            send_line(send1, recv1, send1_sem, recv1_sem, part, step)
            return carry

        lax.fori_loop(0, lines, pool_step, 0)
        recv1[part, me] = send1[part, me]

    ordered = jnp.concatenate([ids_col[part].reshape(part_rows, 8) for part in range(PARTS)], axis=0)
    ids_row[...] = ordered.T

    def mix_step(b, carry):
        square = grad_ref[pl.ds(b, shards, stride=PARTS * deep), :]
        square = square + square.T
        first, second, third = split_three(square)
        mix[b] = jnp.concatenate([first, second, third], axis=0)
        return carry

    lax.fori_loop(0, PARTS * deep, mix_step, 0)

    row_block = 128 if rows % 128 == 0 else rows

    def hit_step(block, carry):
        base = pl.multiple_of(block * row_block, row_block)
        row = lax.broadcasted_iota(jnp.int32, (row_block, samples), 0) + base
        total = jnp.zeros((row_block, samples), jnp.float32)
        for j in range(slots):
            total = total + jnp.where(ids_row[j:j + 1, :] == row, 1.0, 0.0)
        hit[pl.ds(base, row_block), :] = total.astype(jnp.bfloat16)
        return carry

    lax.fori_loop(0, rows // row_block, hit_step, 0)
    state_col[...] = jnp.broadcast_to(state_ref[...], (128, rows)).T

    acc = jnp.int32(0)
    for h in range(groups):
        starts[h] = acc
        acc = acc + counts_ref[h]

    def pick_step(k, carry):
        other = dest(k)
        place = lax.broadcasted_iota(jnp.int32, (CAP, rows), 0)
        row = lax.broadcasted_iota(jnp.int32, (CAP, rows), 1)
        goal = jnp.where(place < counts_ref[other], place + starts[other], -1)
        pick[k] = jnp.where(goal == row, 1.0, 0.0).astype(jnp.bfloat16)
        return carry

    lax.fori_loop(0, groups, pick_step, 0)

    for part in range(PARTS):
        all_blocks(send1, recv1, send1_sem, recv1_sem, part).wait_recv()
        block = recv1[part].reshape(part_rows, width).astype(jnp.float32)
        in_left[...] = block[:, :half]
        in_right[...] = block[:, half:]

        def sample_step(i, carry, part=part):
            inner = jnp.concatenate(
                [in_left[pl.ds(i, shards, stride=deep), :], in_right[pl.ds(i, shards, stride=deep), :]],
                axis=1,
            ).astype(jnp.bfloat16)
            product = jnp.dot(mix[part * deep + i], inner, preferred_element_type=jnp.float32)
            outer = product[0:shards] + product[shards:2 * shards] + product[2 * shards:3 * shards]
            out_left[pl.ds(i, shards, stride=deep), :] = outer[:, :half]
            out_right[pl.ds(i, shards, stride=deep), :] = outer[:, half:]
            return carry

        lax.fori_loop(0, deep, sample_step, 0)
        both = jnp.concatenate([out_left[...], out_right[...]], axis=1)
        send2[part] = both.astype(jnp.bfloat16).reshape(shards, deep, width)

        def back_step(step, carry, part=part):
            send_line(send2, recv2, send2_sem, recv2_sem, part, step)
            return carry

        lax.fori_loop(0, lines, back_step, 0)
        recv2[part, me] = send2[part, me]

    all_blocks(send2, recv2, send2_sem, recv2_sem, 0).wait_recv()
    grads[...] = jnp.dot(
        hit[:, 0:part_rows], recv2[0].reshape(part_rows, width), preferred_element_type=jnp.float32
    )
    all_blocks(send2, recv2, send2_sem, recv2_sem, 1).wait_recv()

    def update_step(block, carry):
        base = pl.multiple_of(block * row_block, row_block)
        here = pl.ds(base, row_block)
        row_grads = grads[here, :] + jnp.dot(
            hit[here, part_rows:2 * part_rows],
            recv2[1].reshape(part_rows, width),
            preferred_element_type=jnp.float32,
        )
        square = jnp.sum(row_grads * row_grads, axis=-1, keepdims=True) * (1.0 / width)
        new_state = state_col[here, :] + square
        step = learn_rate / (jnp.sqrt(new_state) + epsilon)
        new_rows = table_ref[here, :] - row_grads * step[:, 0:1]
        new_table_ref[here, :] = new_rows
        scale = jnp.maximum(jnp.max(jnp.abs(new_rows), axis=-1, keepdims=True), 1e-30)
        whole = jnp.round(new_rows * (TOP / scale))
        upper = jnp.round(whole * (1.0 / 256.0))
        coded[here, 0:width] = upper.astype(jnp.bfloat16)
        coded[here, width:2 * width] = (whole - upper * 256.0).astype(jnp.bfloat16)
        lane = lax.broadcasted_iota(jnp.int32, (row_block, 128), 1)
        side_col[here, :] = jnp.where(lane == 0, new_state, scale * (1.0 / TOP))
        return carry

    lax.fori_loop(0, rows // row_block, update_step, 0)

    def code_copy(other):
        return pltpu.make_async_remote_copy(
            src_ref=code_send.at[other],
            dst_ref=code_recv.at[group],
            send_sem=code_sem.at[0],
            recv_sem=code_sem.at[1],
            device_id=(other, me),
            device_id_type=MESH,
        )

    def side_copy(other):
        return pltpu.make_async_remote_copy(
            src_ref=side_send.at[other],
            dst_ref=side_recv.at[group],
            send_sem=side_sem.at[0],
            recv_sem=side_sem.at[1],
            device_id=(other, me),
            device_id_type=MESH,
        )

    side_rows = side_col[...].T[0:8]
    side_parts = jnp.concatenate(split_three(side_rows), axis=0)
    band = 4 if groups % 4 == 0 else groups

    def pack_step(block, carry):
        select = pick[pl.ds(block * band, band)].reshape(band * CAP, rows)
        both = jnp.dot(select, coded[...], preferred_element_type=jnp.float32)
        values = both[:, :width] * 256.0 + both[:, width:]
        values = values.astype(jnp.int32).astype(jnp.int16).reshape(band, CAP, width)
        aside = lax.dot_general(
            side_parts, select, (((1,), (1,)), ((), ())), preferred_element_type=jnp.float32
        )
        aside = aside[0:8] + aside[8:16] + aside[16:24]
        for turn in range(band):
            k = block * band + turn
            other = dest(k)
            code_send[other] = values[turn]
            side_send[other, :, 0:CAP] = aside[0:2, turn * CAP:(turn + 1) * CAP]

            @pl.when(k != wing)
            def _():
                code_copy(other).start()
                side_copy(other).start()

        return carry

    side_send[...] = jnp.zeros(side_send.shape, jnp.float32)
    lax.fori_loop(0, groups // band, pack_step, 0)
    code_recv[group] = code_send[group]
    side_recv[group] = side_send[group]

    new_state_ref[...] = side_rows[0:1]

    others = pl.ds(0, groups - 1)
    next_group = (group + 1) % groups
    all_codes = pltpu.make_async_remote_copy(
        src_ref=code_send.at[others],
        dst_ref=code_recv.at[others],
        send_sem=code_sem.at[0],
        recv_sem=code_sem.at[1],
        device_id=(next_group, me),
        device_id_type=MESH,
    )
    all_sides = pltpu.make_async_remote_copy(
        src_ref=side_send.at[others],
        dst_ref=side_recv.at[others],
        send_sem=side_sem.at[0],
        recv_sem=side_sem.at[1],
        device_id=(next_group, me),
        device_id_type=MESH,
    )
    for part in range(PARTS):
        all_blocks(send1, recv1, send1_sem, recv1_sem, part).wait_send()
        all_blocks(send2, recv2, send2_sem, recv2_sem, part).wait_send()
    all_sides.wait_recv()
    side_ref[...] = side_recv[...]
    all_codes.wait_recv()
    code_ref[...] = code_recv[...]
    all_sides.wait_send()
    all_codes.wait_send()


def on_device(table, row_state, bag_ids, bag_lengths, interaction_grad, move_rows):
    groups = lax.axis_size("group")
    shards = lax.axis_size("shard")
    line = 6 if shards % 6 == 0 else 2
    rows, width = table.shape[2:]
    slots, samples = bag_ids.shape[2:]
    deep = samples // shards // PARTS
    squares = jnp.transpose(interaction_grad[0], (0, 2, 1)).reshape(samples, shards)
    in_vmem = pl.BlockSpec(memory_space=pltpu.VMEM)
    in_smem = pl.BlockSpec(memory_space=pltpu.SMEM)
    blocks = (PARTS, shards, deep, width)
    bf16, f32, i32, i16 = jnp.bfloat16, jnp.float32, jnp.int32, jnp.int16
    lanes = (shards * deep, width // 2)
    pair = pltpu.SemaphoreType.DMA((2,))
    new_table, new_state, code, side = pl.pallas_call(
        functools.partial(bag_kernel, groups, shards, line),
        out_shape=(
            jax.ShapeDtypeStruct((rows, width), f32),
            jax.ShapeDtypeStruct((1, rows), f32),
            jax.ShapeDtypeStruct((groups, CAP, width), i16),
            jax.ShapeDtypeStruct((groups, 2, 128), f32),
        ),
        in_specs=[in_vmem] * 5 + [in_smem],
        out_specs=(in_vmem,) * 4,
        scratch_shapes=[
            pltpu.VMEM((PARTS, shards, deep, 8), i32),
            pltpu.VMEM((8, samples), i32),
            pltpu.VMEM((rows, 3 * width), bf16),
            pltpu.VMEM((rows, samples), bf16),
            pltpu.VMEM((PARTS * deep, 3 * shards, shards), bf16),
            pltpu.VMEM(blocks, bf16),
            pltpu.VMEM(blocks, bf16),
            pltpu.VMEM(blocks, bf16),
            pltpu.VMEM(blocks, bf16),
            pltpu.VMEM(lanes, f32),
            pltpu.VMEM(lanes, f32),
            pltpu.VMEM(lanes, f32),
            pltpu.VMEM(lanes, f32),
            pltpu.VMEM((rows, width), f32),
            pltpu.VMEM((rows, 128), f32),
            pltpu.VMEM((rows, 2 * width), bf16),
            pltpu.VMEM((rows, 128), f32),
            pltpu.VMEM((groups, CAP, rows), bf16),
            pltpu.VMEM((groups, CAP, width), i16),
            pltpu.VMEM((groups, CAP, width), i16),
            pltpu.VMEM((groups, 2, 128), f32),
            pltpu.VMEM((groups, 2, 128), f32),
            pltpu.SMEM((groups,), i32),
            pair, pair, pair, pair, pair, pair,
        ],
        compiler_params=pltpu.CompilerParams(
            collective_id=0, has_side_effects=True, vmem_limit_bytes=48 * 1024 * 1024
        ),
        cost_estimate=pl.CostEstimate(
            flops=8 * samples * rows * width, bytes_accessed=6 * rows * width * 4, transcendentals=0
        ),
    )(
        table[0, 0],
        row_state[0],
        bag_ids[0, 0],
        bag_lengths[0],
        squares,
        move_rows[0, 0],
    )
    arrived = code.astype(jnp.float32) * side[:, 1, :CAP, None]
    return (
        new_table[None, None],
        new_state[None],
        arrived.reshape(1, groups, 1, CAP, width),
        side[:, 0, :CAP].reshape(1, groups, 1, CAP),
    )


def solution(mesh):
    in_specs = (
        P("group", "shard", None, None),
        P("group", "shard", None),
        P("group", "shard", None, None),
        P("group", "shard", None),
        P("group", None, None, "shard"),
        P("group", "shard", None),
    )
    out_specs = (
        P("group", "shard", None, None),
        P("group", "shard", None),
        P("group", None, "shard", None, None),
        P("group", None, "shard", None),
    )
    return jax.shard_map(
        on_device, mesh=mesh, in_specs=in_specs, out_specs=out_specs, check_vma=False
    )
```

time: 246 us -> 111 us (0.45)
  the two profiles are of different devices: /device:TPU:72 before, /device:TPU:1 now
where the time goes in v2:
time: 111 us
  Pallas kernels  103 us (93%)
  local copies, waits for them, and re-layouts  5.95 us (5%)
  other arithmetic  1.18 us (1%)
    pallas_call x1, Pallas kernels, on_device(): pl.pallas_call(functools.partial(bag_kernel, groups, shards, line), out_s...  103 us
    unnamed x15, local copies, waits for them, and re-layouts  5.95 us

profile of v2, /device:TPU:1, one launch (start us, length us, event | category | flops | bytes accessed | tf_op | source)
XLA Modules:
  0.0 110.6 jit_solution(13878113010093547030)
XLA Ops:
  0.6 0.0 copy-start.3
  0.6 0.0 copy-start.4
  0.7 0.0 copy-start.5
  0.7 0.7 copy-done.3
  1.3 0.0 copy-done.4
  1.3 0.0 copy-done.5
  1.3 0.0 copy-start
  1.3 1.2 %copy-done = f32[1,1,1024,256]{3,2,1,0:T(8,128)S(1)} copy-done((f32[1,1,1024,256]{3,2,1,0:T(8,128)S(1)}, f32[1,1,1024,256]{3,2,1,0:T(8,128)}, u32[]{:S(2)}) %copy-start) | copy-done | bytes 1048600
  2.6 0.0 copy-start.1
  2.6 1.1 %copy-done.1 = f32[1,48,48,32]{2,3,1,0:T(8,128)S(1)} copy-done((f32[1,48,48,32]{2,3,1,0:T(8,128)S(1)}, f32[1,48,48,32]{2,3,1,0:T(8,128)}, u32[]{:S(2)}) %copy-start.1) | copy-done | bytes 294936
  3.7 0.0 copy-start.2
  3.7 0.7 copy-done.2
  4.4 102.8 %shard_map.93 = (f32[1024,256]{1,0:T(8,128)S(1)}, f32[1,1024]{1,0:T(1,128)S(1)}, s16[16,64,256]{2,1,0:T(8,128)(2,1)S(1)}, f32[16,2,128]{2,1,0:T(2,128)S(1)}) custom-call(f32[1024,256]{1,0:T(8,128)S(1)} %bitcast.23, f32[1,1024]{1,0:T(1,128)S(1)} %bitcast.27, s32[4,1536]{1,0:T(4,128)S(1)} %bitcast.25, s32[1,1536]{1,0:T(1,128)S(1)} %bitcast.26, ...), custom_call_target="tpu_custom_call" | custom-call | flops 3221225472 | bytes 6291456 | tf_op jit(solution)/shard_map/pallas_call | solution.py:330
  107.3 0.6 slice_bitcast_fusion
  107.9 1.2 %multiply_bitcast_fusion = f32[1,16,1,64,256]{4,3,2,1,0:T(8,128)} fusion(s16[16,64,256]{2,1,0:T(8,128)(2,1)S(1)} %get-tuple-element.10, f32[16,64]{1,0:T(8,128)S(1)} %bitcast.29), kind=kLoop, calls=%fused_computation | loop fusion | flops 524288 | bytes 1576960
  109.0 1.0 copy.14
  110.0 0.6 copy.15
Async XLA Ops:
  0.6 0.7 copy-start.3
  0.6 0.7 copy-start.4
  0.7 0.7 copy-start.5
  1.3 1.2 %copy-start = (f32[1,1,1024,256]{3,2,1,0:T(8,128)S(1)}, f32[1,1,1024,256]{3,2,1,0:T(8,128)}, u32[]{:S(2)}) copy-start(f32[1,1,1024,256]{3,2,1,0:T(8,128)} %param.6) | copy-start | bytes 3145732
  2.6 1.1 %copy-start.1 = (f32[1,48,48,32]{2,3,1,0:T(8,128)S(1)}, f32[1,48,48,32]{2,3,1,0:T(8,128)}, u32[]{:S(2)}) copy-start(f32[1,48,48,32]{2,3,1,0:T(8,128)} %param.10) | copy-start | bytes 884740
  3.7 0.7 copy-start.2

commit v3 on v2

v3 whole, which is shorter than its diff:
```python
import functools

import jax
import jax.numpy as jnp
from jax import lax
from jax.experimental import pallas as pl
from jax.experimental.pallas import tpu as pltpu
from jax.sharding import PartitionSpec as P

MESH = pl.DeviceIdType.MESH
CAP = 64
PARTS = 2
TOP = 32767.0
VMEM_BYTES = 60 * 1024 * 1024

learn_rate = 0.05
epsilon = 1e-08


def split_three(values):
    high = values.astype(jnp.bfloat16)
    rest = values - high.astype(jnp.float32)
    middle = rest.astype(jnp.bfloat16)
    low = (rest - middle.astype(jnp.float32)).astype(jnp.bfloat16)
    return high, middle, low


def bag_kernel(
    groups, shards, line,
    table_hbm, state_hbm, ids_hbm, len_hbm, grad_hbm, counts_hbm,
    new_table_hbm, new_state_hbm, code_recv, side_recv,
    table_ref, state_ref, ids_ref, len_ref, grad_ref, counts_ref,
    ids_col, ids_row, parts, state_parts, hit, picked_hit, mix, send1, recv1, send2, recv2,
    in_left, in_right, out_left, out_right, grads, picked_grads, picked_table, picked_state,
    state_col, new_col, new_table_ref, new_state_ref, code_send, side_send, starts,
    load_sem, store_sem, send1_sem, recv1_sem, send2_sem, recv2_sem, code_sem, side_sem,
):
    rows, width = table_ref.shape
    slots, samples = ids_ref.shape
    deep = samples // shards // PARTS
    half = width // 2
    part_rows = shards * deep
    lines = shards // line
    group = lax.axis_index("group")
    me = lax.axis_index("shard")
    my_line = me // line
    my_spot = me % line
    wing = groups // 2
    my_wing = group // wing
    my_place = group % wing

    loads = [
        pltpu.make_async_copy(source, target, load_sem.at[i])
        for i, (source, target) in enumerate((
            (ids_hbm, ids_ref),
            (len_hbm, len_ref),
            (table_hbm, table_ref),
            (grad_hbm, grad_ref),
            (state_hbm, state_ref),
            (counts_hbm, counts_ref),
        ))
    ]
    for load in loads:
        load.start()

    def dest(k):
        return ((my_wing + 1 + k // wing) % 2) * wing + (my_place + k) % wing

    barrier = pltpu.get_barrier_semaphore()

    def greet_shard(k, carry):
        pl.semaphore_signal(
            barrier, inc=1, device_id=(group, (me + k) % shards), device_id_type=MESH
        )
        return carry

    def greet_group(k, carry):
        pl.semaphore_signal(
            barrier, inc=1, device_id=((group + k) % groups, me), device_id_type=MESH
        )
        return carry

    lax.fori_loop(1, shards, greet_shard, 0)
    lax.fori_loop(1, groups, greet_group, 0)

    def block_copy(source, target, send_sem, recv_sem, part, other):
        return pltpu.make_async_remote_copy(
            src_ref=source.at[part, other],
            dst_ref=target.at[part, me],
            send_sem=send_sem.at[part],
            recv_sem=recv_sem.at[part],
            device_id=(group, other),
            device_id_type=MESH,
        )

    def all_blocks(source, target, send_sem, recv_sem, part):
        return pltpu.make_async_remote_copy(
            src_ref=source.at[part, pl.ds(0, shards - 1)],
            dst_ref=target.at[part, pl.ds(0, shards - 1)],
            send_sem=send_sem.at[part],
            recv_sem=recv_sem.at[part],
            device_id=(group, (me + 1) % shards),
            device_id_type=MESH,
        )

    def send_line(source, target, send_sem, recv_sem, part, step, first_turn):
        first = ((my_line + step) % lines) * line
        for turn in range(first_turn, line):
            other = first + (my_spot + turn) % line
            block_copy(source, target, send_sem, recv_sem, part, other).start()

    loads[0].wait()
    loads[1].wait()
    slot = lax.broadcasted_iota(jnp.int32, (slots, samples), 0)
    live = jnp.where(slot < len_ref[...], ids_ref[...], -1)
    live = jnp.concatenate([live, jnp.full((8 - slots, samples), -1, jnp.int32)], axis=0)
    columns = live.T.reshape(shards, PARTS, deep, 8)
    for part in range(PARTS):
        ids_col[part] = columns[:, part]

    loads[2].wait()
    high, middle, low = split_three(table_ref[...])
    parts[:, 0:width] = high
    parts[:, width:2 * width] = middle
    parts[:, 2 * width:3 * width] = low

    def pool_line(part, step):
        first = ((my_line + step) % lines) * line
        column = ids_col[part, pl.ds(first, line)].reshape(line * deep, 8)
        lane = lax.broadcasted_iota(jnp.int32, (line * deep, rows), 1)
        total = jnp.zeros((line * deep, rows), jnp.float32)
        for j in range(slots):
            total = total + jnp.where(column[:, j:j + 1] == lane, 1.0, 0.0)
        product = jnp.dot(
            total.astype(jnp.bfloat16), parts[...], preferred_element_type=jnp.float32
        )
        pooled = product[:, 0:width] + product[:, width:2 * width]
        pooled = pooled + product[:, 2 * width:3 * width]
        send1[part, pl.ds(first, line)] = pooled.astype(jnp.bfloat16).reshape(line, deep, width)

    for part in range(PARTS):
        def pool_step(step, carry, part=part):
            pool_line(part, step)
            send_line(send1, recv1, send1_sem, recv1_sem, part, step, 0)
            return carry

        pool_line(part, 0)
        if part == 0:
            pl.semaphore_wait(barrier, shards + groups - 2)
        send_line(send1, recv1, send1_sem, recv1_sem, part, 0, 1)
        lax.fori_loop(1, lines, pool_step, 0)
        recv1[part, me] = send1[part, me]

    loads[3].wait()

    def mix_step(b, carry):
        square = grad_ref[pl.ds(b, shards, stride=PARTS * deep), :]
        square = square + square.T
        first, second, third = split_three(square)
        mix[b] = jnp.concatenate([first, second, third], axis=0)
        return carry

    lax.fori_loop(0, PARTS * deep, mix_step, 0)

    def mix_part(part):
        all_blocks(send1, recv1, send1_sem, recv1_sem, part).wait_recv()
        block = recv1[part].reshape(part_rows, width).astype(jnp.float32)
        in_left[...] = block[:, :half]
        in_right[...] = block[:, half:]

        def sample_step(i, carry):
            inner = jnp.concatenate(
                [in_left[pl.ds(i, shards, stride=deep), :], in_right[pl.ds(i, shards, stride=deep), :]],
                axis=1,
            ).astype(jnp.bfloat16)
            product = jnp.dot(mix[part * deep + i], inner, preferred_element_type=jnp.float32)
            outer = product[0:shards] + product[shards:2 * shards] + product[2 * shards:3 * shards]
            out_left[pl.ds(i, shards, stride=deep), :] = outer[:, :half]
            out_right[pl.ds(i, shards, stride=deep), :] = outer[:, half:]
            return carry

        lax.fori_loop(0, deep, sample_step, 0)
        both = jnp.concatenate([out_left[...], out_right[...]], axis=1)
        send2[part] = both.astype(jnp.bfloat16).reshape(shards, deep, width)

        def back_step(step, carry):
            send_line(send2, recv2, send2_sem, recv2_sem, part, step, 0)
            return carry

        send_line(send2, recv2, send2_sem, recv2_sem, part, 0, 1)
        lax.fori_loop(1, lines, back_step, 0)
        recv2[part, me] = send2[part, me]

    mix_part(0)

    ordered = jnp.concatenate([ids_col[part].reshape(part_rows, 8) for part in range(PARTS)], axis=0)
    ids_row[...] = ordered.T
    loads[4].wait()
    loads[5].wait()
    state_col[...] = jnp.broadcast_to(state_ref[...], (128, rows)).T
    acc = jnp.int32(0)
    for h in range(groups):
        starts[h] = acc
        acc = acc + counts_ref[0, h]
    lane = lax.broadcasted_iota(jnp.int32, (rows, 128), 1)
    first, second, third = (piece.astype(jnp.float32) for piece in split_three(state_col[...]))
    state_parts[...] = jnp.where(
        lane == 0, first, jnp.where(lane == 1, second, jnp.where(lane == 2, third, 0.0))
    ).astype(jnp.bfloat16)

    band = 4 if groups % 4 == 0 else groups
    tall = band * CAP

    def goals(block):
        place = lax.broadcasted_iota(jnp.int32, (CAP, 128), 0)
        pieces = []
        for turn in range(band):
            other = dest(block * band + turn)
            pieces.append(jnp.where(place < counts_ref[0, other], place + starts[other], -2))
        return jnp.concatenate(pieces, axis=0)[:, 0:1]

    def count_hits(goal, size):
        total = jnp.zeros((size, samples), jnp.float32)
        for j in range(slots):
            total = total + jnp.where(ids_row[j:j + 1, :] == goal, 1.0, 0.0)
        return total.astype(jnp.bfloat16)

    def pick_step(block, carry):
        here = pl.ds(pl.multiple_of(block * tall, tall), tall)
        goal = goals(block)
        for piece in range(2):
            span = slice(piece * tall // 2, (piece + 1) * tall // 2)
            at = pl.ds(pl.multiple_of(block * tall + piece * tall // 2, tall // 2), tall // 2)
            picked_hit[at, :] = count_hits(goal[span], tall // 2)
        pick = jnp.where(
            goal == lax.broadcasted_iota(jnp.int32, (tall, rows), 1), 1.0, 0.0
        ).astype(jnp.bfloat16)
        product = jnp.dot(pick, parts[...], preferred_element_type=jnp.float32)
        both = product[:, 0:width] + product[:, width:2 * width]
        picked_table[here, :] = both + product[:, 2 * width:3 * width]
        product = jnp.dot(pick, state_parts[...], preferred_element_type=jnp.float32)
        total = (product[:, 0:1] + product[:, 1:2]) + product[:, 2:3]
        picked_state[here, :] = jnp.broadcast_to(total, (tall, 128))
        return carry

    lax.fori_loop(0, groups // band, pick_step, 0)

    mix_part(1)

    row_block = 128 if rows % 128 == 0 else rows

    def hit_step(block, carry):
        base = pl.multiple_of(block * row_block, row_block)
        row = lax.broadcasted_iota(jnp.int32, (row_block, samples), 0) + base
        hit[pl.ds(base, row_block), :] = count_hits(row, row_block)
        return carry

    lax.fori_loop(0, rows // row_block, hit_step, 0)
    side_send[...] = jnp.zeros(side_send.shape, jnp.float32)

    all_blocks(send2, recv2, send2_sem, recv2_sem, 0).wait_recv()
    returned = recv2[0].reshape(part_rows, width)
    picked_grads[...] = jnp.dot(
        picked_hit[:, 0:part_rows], returned, preferred_element_type=jnp.float32
    )
    grads[...] = jnp.dot(hit[:, 0:part_rows], returned, preferred_element_type=jnp.float32)

    def adagrad(old_rows, old_state, row_grads):
        square = jnp.sum(row_grads * row_grads, axis=-1, keepdims=True) * (1.0 / width)
        new_state = old_state + square
        step = learn_rate / (jnp.sqrt(new_state) + epsilon)
        return old_rows - row_grads * step[:, 0:1], new_state

    def code_copy(other):
        return pltpu.make_async_remote_copy(
            src_ref=code_send.at[other],
            dst_ref=code_recv.at[group],
            send_sem=code_sem.at[0],
            recv_sem=code_sem.at[1],
            device_id=(other, me),
            device_id_type=MESH,
        )

    def side_copy(other):
        return pltpu.make_async_remote_copy(
            src_ref=side_send.at[other],
            dst_ref=side_recv.at[group],
            send_sem=side_sem.at[0],
            recv_sem=side_sem.at[1],
            device_id=(other, me),
            device_id_type=MESH,
        )

    all_blocks(send2, recv2, send2_sem, recv2_sem, 1).wait_recv()

    def pack_step(block, carry):
        here = pl.ds(pl.multiple_of(block * tall, tall), tall)
        row_grads = picked_grads[here, :] + jnp.dot(
            picked_hit[here, part_rows:2 * part_rows],
            recv2[1].reshape(part_rows, width),
            preferred_element_type=jnp.float32,
        )
        new_rows, new_state = adagrad(picked_table[here, :], picked_state[here, :], row_grads)
        scale = jnp.maximum(jnp.max(jnp.abs(new_rows), axis=-1, keepdims=True), 1e-30)
        values = jnp.round(new_rows * (TOP / scale))
        values = values.astype(jnp.int32).astype(jnp.int16).reshape(band, CAP, width)
        at = lax.broadcasted_iota(jnp.int32, (tall, 128), 1)
        aside = jnp.where(at == 0, new_state, scale * (1.0 / TOP)).T
        for turn in range(band):
            k = block * band + turn
            other = dest(k)
            code_send[other] = values[turn]
            side_send[other, :, 0:CAP] = aside[0:2, turn * CAP:(turn + 1) * CAP]

            @pl.when(k != wing)
            def _():
                code_copy(other).start()
                side_copy(other).start()

        return carry

    lax.fori_loop(0, groups // band, pack_step, 0)
    stores = [
        pltpu.make_async_copy(source, target, store_sem.at[i])
        for i, (source, target) in enumerate((
            (code_send.at[group], code_recv.at[group]),
            (side_send.at[group], side_recv.at[group]),
            (new_table_ref, new_table_hbm),
            (new_state_ref, new_state_hbm),
        ))
    ]
    stores[0].start()
    stores[1].start()

    def update_step(block, carry):
        base = pl.multiple_of(block * row_block, row_block)
        here = pl.ds(base, row_block)
        row_grads = grads[here, :] + jnp.dot(
            hit[here, part_rows:2 * part_rows],
            recv2[1].reshape(part_rows, width),
            preferred_element_type=jnp.float32,
        )
        new_rows, new_state = adagrad(table_ref[here, :], state_col[here, :], row_grads)
        new_table_ref[here, :] = new_rows
        new_col[here, :] = new_state
        return carry

    lax.fori_loop(0, rows // row_block, update_step, 0)
    stores[2].start()
    new_state_ref[...] = new_col[...].T[0:1]
    stores[3].start()

    others = pl.ds(0, groups - 1)
    next_group = (group + 1) % groups
    all_codes = pltpu.make_async_remote_copy(
        src_ref=code_send.at[others],
        dst_ref=code_recv.at[others],
        send_sem=code_sem.at[0],
        recv_sem=code_sem.at[1],
        device_id=(next_group, me),
        device_id_type=MESH,
    )
    all_sides = pltpu.make_async_remote_copy(
        src_ref=side_send.at[others],
        dst_ref=side_recv.at[others],
        send_sem=side_sem.at[0],
        recv_sem=side_sem.at[1],
        device_id=(next_group, me),
        device_id_type=MESH,
    )
    for part in range(PARTS):
        all_blocks(send1, recv1, send1_sem, recv1_sem, part).wait_send()
        all_blocks(send2, recv2, send2_sem, recv2_sem, part).wait_send()
    for store in stores:
        store.wait()
    all_sides.wait_send()
    all_codes.wait_send()
    all_sides.wait_recv()
    all_codes.wait_recv()


def finish_kernel(
    table_hbm, state_hbm, code_hbm, side_hbm,
    new_table_ref, new_state_ref, arrived_ref, arrived_state_ref,
    code_ref, side_ref, decoded, states, in_sems, out_sems,
):
    groups = code_ref.shape[0]
    pieces = 4
    band = groups // pieces
    side_in = pltpu.make_async_copy(side_hbm, side_ref, in_sems.at[0])
    side_in.start()
    codes_in = []
    for block in range(pieces):
        here = pl.ds(block * band, band)
        copy = pltpu.make_async_copy(code_hbm.at[here], code_ref.at[here], in_sems.at[1 + block])
        copy.start()
        codes_in.append(copy)
    copies = [
        pltpu.make_async_copy(table_hbm, new_table_ref.at[0, 0], out_sems.at[0]),
        pltpu.make_async_copy(state_hbm, new_state_ref.at[0], out_sems.at[1]),
        pltpu.make_async_copy(states, arrived_state_ref, out_sems.at[2]),
    ]
    copies[0].start()
    copies[1].start()
    side_in.wait()
    states[0] = side_ref[:, 0:1, 0:CAP]
    copies[2].start()
    scales = side_ref[:, 1, :].T
    for block in range(pieces):
        codes_in[block].wait()
        for turn in range(band):
            h = block * band + turn
            decoded[0, h, 0] = code_ref[h].astype(jnp.float32) * scales[0:CAP, h:h + 1]
        here = pl.ds(block * band, band)
        copy = pltpu.make_async_copy(
            decoded.at[0, here], arrived_ref.at[0, here], out_sems.at[3 + block]
        )
        copy.start()
        copies.append(copy)
    for copy in copies:
        copy.wait()


def on_device(table, row_state, bag_ids, bag_lengths, interaction_grad, move_rows):
    groups = lax.axis_size("group")
    shards = lax.axis_size("shard")
    line = 6 if shards % 6 == 0 else 2
    rows, width = table.shape[2:]
    slots, samples = bag_ids.shape[2:]
    deep = samples // shards // PARTS
    squares = jnp.transpose(interaction_grad[0], (0, 2, 1)).reshape(samples, shards)
    in_hbm = pl.BlockSpec(memory_space=pltpu.HBM)
    blocks = (PARTS, shards, deep, width)
    bf16, f32, i32, i16 = jnp.bfloat16, jnp.float32, jnp.int32, jnp.int16
    lanes = (shards * deep, width // 2)
    moved = groups * CAP
    pair = pltpu.SemaphoreType.DMA((2,))
    new_table, new_state, code, side = pl.pallas_call(
        functools.partial(bag_kernel, groups, shards, line),
        name="bags",
        out_shape=(
            jax.ShapeDtypeStruct((rows, width), f32),
            jax.ShapeDtypeStruct((1, rows), f32),
            jax.ShapeDtypeStruct((groups, CAP, width), i16),
            jax.ShapeDtypeStruct((groups, 2, 128), f32),
        ),
        in_specs=[in_hbm] * 6,
        out_specs=(in_hbm,) * 4,
        scratch_shapes=[
            pltpu.VMEM((rows, width), f32),
            pltpu.VMEM((1, rows), f32),
            pltpu.VMEM((slots, samples), i32),
            pltpu.VMEM((1, samples), i32),
            pltpu.VMEM((samples, shards), f32),
            pltpu.SMEM((1, groups), i32),
            pltpu.VMEM((PARTS, shards, deep, 8), i32),
            pltpu.VMEM((8, samples), i32),
            pltpu.VMEM((rows, 3 * width), bf16),
            pltpu.VMEM((rows, 128), bf16),
            pltpu.VMEM((rows, samples), bf16),
            pltpu.VMEM((moved, samples), bf16),
            pltpu.VMEM((PARTS * deep, 3 * shards, shards), bf16),
            pltpu.VMEM(blocks, bf16),
            pltpu.VMEM(blocks, bf16),
            pltpu.VMEM(blocks, bf16),
            pltpu.VMEM(blocks, bf16),
            pltpu.VMEM(lanes, f32),
            pltpu.VMEM(lanes, f32),
            pltpu.VMEM(lanes, f32),
            pltpu.VMEM(lanes, f32),
            pltpu.VMEM((rows, width), f32),
            pltpu.VMEM((moved, width), f32),
            pltpu.VMEM((moved, width), f32),
            pltpu.VMEM((moved, 128), f32),
            pltpu.VMEM((rows, 128), f32),
            pltpu.VMEM((rows, 128), f32),
            pltpu.VMEM((rows, width), f32),
            pltpu.VMEM((1, rows), f32),
            pltpu.VMEM((groups, CAP, width), i16),
            pltpu.VMEM((groups, 2, 128), f32),
            pltpu.SMEM((groups,), i32),
            pltpu.SemaphoreType.DMA((6,)),
            pltpu.SemaphoreType.DMA((4,)),
            pair, pair, pair, pair, pair, pair,
        ],
        compiler_params=pltpu.CompilerParams(
            collective_id=0, has_side_effects=True, vmem_limit_bytes=VMEM_BYTES
        ),
        cost_estimate=pl.CostEstimate(
            flops=12 * samples * rows * width, bytes_accessed=6 * rows * width * 4, transcendentals=0
        ),
    )(
        table[0, 0],
        row_state[0],
        bag_ids[0, 0],
        bag_lengths[0],
        squares,
        move_rows[0],
    )
    return pl.pallas_call(
        finish_kernel,
        name="finish",
        out_shape=(
            jax.ShapeDtypeStruct((1, 1, rows, width), f32),
            jax.ShapeDtypeStruct((1, 1, rows), f32),
            jax.ShapeDtypeStruct((1, groups, 1, CAP, width), f32),
            jax.ShapeDtypeStruct((1, groups, 1, CAP), f32),
        ),
        in_specs=[in_hbm] * 4,
        out_specs=(in_hbm,) * 4,
        scratch_shapes=[
            pltpu.VMEM((groups, CAP, width), i16),
            pltpu.VMEM((groups, 2, 128), f32),
            pltpu.VMEM((1, groups, 1, CAP, width), f32),
            pltpu.VMEM((1, groups, 1, CAP), f32),
            pltpu.SemaphoreType.DMA((5,)),
            pltpu.SemaphoreType.DMA((7,)),
        ],
        compiler_params=pltpu.CompilerParams(vmem_limit_bytes=VMEM_BYTES),
        cost_estimate=pl.CostEstimate(
            flops=rows * width, bytes_accessed=10 * rows * width, transcendentals=0
        ),
    )(new_table, new_state, code, side)


def solution(mesh):
    in_specs = (
        P("group", "shard", None, None),
        P("group", "shard", None),
        P("group", "shard", None, None),
        P("group", "shard", None),
        P("group", None, None, "shard"),
        P("group", "shard", None),
    )
    out_specs = (
        P("group", "shard", None, None),
        P("group", "shard", None),
        P("group", None, "shard", None, None),
        P("group", None, "shard", None),
    )
    return jax.shard_map(
        on_device, mesh=mesh, in_specs=in_specs, out_specs=out_specs, check_vma=False
    )
```

time: 111 us -> 132 us (1.19)
  Pallas kernels: 103 us -> 131 us
  local copies, waits for them, and re-layouts: 5.95 us -> 0 us
    pallas_call x1 -> x2, Pallas kernels: 103 us -> 131 us  [the longest x1 97.5 us: on_device(): pl.pallas_call(functools.partial(bag_kernel, groups, shards, line), name=...]
    unnamed x15 -> x0, local copies, waits for them, and re-layouts: 5.95 us -> none
where the time goes in v3:
time: 132 us; the launch traced here: 131 us
  Pallas kernels  131 us (99%)
    pallas_call x1, Pallas kernels, on_device(): pl.pallas_call(functools.partial(bag_kernel, groups, shards, line), name=...  97.5 us
    pallas_call x1, Pallas kernels, on_device(): pl.pallas_call(finish_kernel, name='finish', out_shape=(jax.ShapeDtypeStr...  33.1 us

profile of v3, /device:TPU:1, one launch (start us, length us, event | category | flops | bytes accessed | tf_op | source)
XLA Modules:
  0.0 131.3 jit_solution(6171911585850911517)
XLA Ops:
  0.6 97.5 %bags.1 = (f32[1024,256]{1,0:T(8,128)}, f32[1,1024]{1,0:T(1,128)}, s16[16,64,256]{2,1,0:T(8,128)(2,1)}, f32[16,2,128]{2,1,0:T(2,128)}) custom-call(f32[1024,256]{1,0:T(8,128)} %bitcast.10, f32[1,1024]{1,0:T(1,128)} %bitcast.14, s32[4,1536]{1,0:T(4,128)} %bitcast.12, s32[1,1536]{1,0:T(1,128)} %bitcast.13, f32[1536,48]{1,0:T(8,128)} %bitcast.11, s32[1,16]{1,0:T(1,128)} %bitcast.15), custom_call_target="tpu_custom_call" | custom-call | flops 4831838208 | bytes 6291456 | tf_op jit(solution)/shard_map/bags/pallas_call | solution.py:438
  98.2 33.1 %finish.1 = (f32[1,1,1024,256]{3,2,1,0:T(8,128)}, f32[1,1,1024]{2,1,0:T(1,128)}, f32[1,16,1,64,256]{4,3,2,1,0:T(8,128)}, f32[1,16,1,64]{3,2,1,0:T(1,128)}) custom-call(f32[1024,256]{1,0:T(8,128)} %get-tuple-element.8.table_hbm, f32[1,1024]{1,0:T(1,128)} %get-tuple-element.9.state_hbm, s16[16,64,256]{2,1,0:T(8,128)(2,1)} %get-tuple-element.10.code_hbm, ...), custom_call_target="tpu_custom_call" | custom-call | flops 262144 | bytes 2621440 | tf_op jit(solution)/shard_map/finish/pallas_call | solution.py:500

commit v4 on v3

--- a/solution.py
+++ b/solution.py
@@ -184,11 +184,25 @@
         send2[part] = both.astype(jnp.bfloat16).reshape(shards, deep, width)
 
         def back_step(step, carry):
-            send_line(send2, recv2, send2_sem, recv2_sem, part, step, 0)
+            if part == 0:
+                send_line(send2, recv2, send2_sem, recv2_sem, part, step, 0)
+                return carry
+            odd = step // lines
+            first = ((my_line + step) % lines) * line
+            for turn in range(line // 2):
+                other = first + ((my_spot // 2 + turn) % (line // 2)) * 2 + odd
+                copy = block_copy(send2, recv2, send2_sem, recv2_sem, part, other)
+                if turn == 0:
+                    pl.when(other != me)(copy.start)
+                else:
+                    copy.start()
             return carry
 
-        send_line(send2, recv2, send2_sem, recv2_sem, part, 0, 1)
-        lax.fori_loop(1, lines, back_step, 0)
+        if part == 0:
+            send_line(send2, recv2, send2_sem, recv2_sem, part, 0, 1)
+            lax.fori_loop(1, lines, back_step, 0)
+        else:
+            lax.fori_loop(0, 2 * lines, back_step, 0)
         recv2[part, me] = send2[part, me]
 
     mix_part(0)
@@ -382,42 +396,55 @@
 def finish_kernel(
     table_hbm, state_hbm, code_hbm, side_hbm,
     new_table_ref, new_state_ref, arrived_ref, arrived_state_ref,
-    code_ref, side_ref, decoded, states, in_sems, out_sems,
+    table_ref, state_ref, code_ref, side_ref, decoded, states, in_sems, out_sems,
 ):
     groups = code_ref.shape[0]
     pieces = 4
     band = groups // pieces
-    side_in = pltpu.make_async_copy(side_hbm, side_ref, in_sems.at[0])
-    side_in.start()
-    codes_in = []
+    rows = table_ref.shape[2] // pieces
+    loads = [
+        pltpu.make_async_copy(side_hbm, side_ref, in_sems.at[0]),
+        pltpu.make_async_copy(state_hbm, state_ref.at[0], in_sems.at[1]),
+    ]
     for block in range(pieces):
         here = pl.ds(block * band, band)
-        copy = pltpu.make_async_copy(code_hbm.at[here], code_ref.at[here], in_sems.at[1 + block])
+        loads.append(
+            pltpu.make_async_copy(code_hbm.at[here], code_ref.at[here], in_sems.at[2 + block])
+        )
+    for block in range(pieces):
+        here = pl.ds(block * rows, rows)
+        loads.append(
+            pltpu.make_async_copy(
+                table_hbm.at[here], table_ref.at[0, 0, here], in_sems.at[2 + pieces + block]
+            )
+        )
+    for load in loads:
+        load.start()
+    stores = []
+
+    def store(source, target):
+        copy = pltpu.make_async_copy(source, target, out_sems.at[len(stores)])
         copy.start()
-        codes_in.append(copy)
-    copies = [
-        pltpu.make_async_copy(table_hbm, new_table_ref.at[0, 0], out_sems.at[0]),
-        pltpu.make_async_copy(state_hbm, new_state_ref.at[0], out_sems.at[1]),
-        pltpu.make_async_copy(states, arrived_state_ref, out_sems.at[2]),
-    ]
-    copies[0].start()
-    copies[1].start()
-    side_in.wait()
+        stores.append(copy)
+
+    loads[0].wait()
     states[0] = side_ref[:, 0:1, 0:CAP]
-    copies[2].start()
+    store(states, arrived_state_ref)
     scales = side_ref[:, 1, :].T
+    loads[1].wait()
+    store(state_ref, new_state_ref)
     for block in range(pieces):
-        codes_in[block].wait()
+        loads[2 + block].wait()
         for turn in range(band):
             h = block * band + turn
             decoded[0, h, 0] = code_ref[h].astype(jnp.float32) * scales[0:CAP, h:h + 1]
         here = pl.ds(block * band, band)
-        copy = pltpu.make_async_copy(
-            decoded.at[0, here], arrived_ref.at[0, here], out_sems.at[3 + block]
-        )
-        copy.start()
-        copies.append(copy)
-    for copy in copies:
+        store(decoded.at[0, here], arrived_ref.at[0, here])
+    for block in range(pieces):
+        here = pl.ds(block * rows, rows)
+        loads[2 + pieces + block].wait()
+        store(table_ref.at[0, 0, here], new_table_ref.at[0, 0, here])
+    for copy in stores:
         copy.wait()
 
 
@@ -509,12 +536,14 @@
         in_specs=[in_hbm] * 4,
         out_specs=(in_hbm,) * 4,
         scratch_shapes=[
+            pltpu.VMEM((1, 1, rows, width), f32),
+            pltpu.VMEM((1, 1, rows), f32),
             pltpu.VMEM((groups, CAP, width), i16),
             pltpu.VMEM((groups, 2, 128), f32),
             pltpu.VMEM((1, groups, 1, CAP, width), f32),
             pltpu.VMEM((1, groups, 1, CAP), f32),
-            pltpu.SemaphoreType.DMA((5,)),
-            pltpu.SemaphoreType.DMA((7,)),
+            pltpu.SemaphoreType.DMA((10,)),
+            pltpu.SemaphoreType.DMA((10,)),
         ],
         compiler_params=pltpu.CompilerParams(vmem_limit_bytes=VMEM_BYTES),
         cost_estimate=pl.CostEstimate(

time: 132 us -> 99.8 us (0.76)
  Pallas kernels: 131 us -> 98.9 us
    pallas_call x1, Pallas kernels: 33.1 us -> 2.57 us  [on_device(): pl.pallas_call(finish_kernel, name='finish', out_shape=(jax.ShapeDtypeStr...]
where the time goes in v4:
time: 99.8 us; the launch traced here: 99.5 us
  Pallas kernels  98.9 us (99%)
    pallas_call x1, Pallas kernels, on_device(): pl.pallas_call(functools.partial(bag_kernel, groups, shards, line), name=...  96.3 us
    pallas_call x1, Pallas kernels, on_device(): pl.pallas_call(finish_kernel, name='finish', out_shape=(jax.ShapeDtypeStr...  2.57 us

profile of v4, /device:TPU:1, one launch (start us, length us, event | category | flops | bytes accessed | tf_op | source)
XLA Modules:
  0.0 99.5 jit_solution(7074629675899889418)
XLA Ops:
  0.6 96.3 %bags.1 = (f32[1024,256]{1,0:T(8,128)}, f32[1,1024]{1,0:T(1,128)}, s16[16,64,256]{2,1,0:T(8,128)(2,1)}, f32[16,2,128]{2,1,0:T(2,128)}) custom-call(f32[1024,256]{1,0:T(8,128)} %bitcast.10, f32[1,1024]{1,0:T(1,128)} %bitcast.14, s32[4,1536]{1,0:T(4,128)} %bitcast.12, s32[1,1536]{1,0:T(1,128)} %bitcast.13, f32[1536,48]{1,0:T(8,128)} %bitcast.11, s32[1,16]{1,0:T(1,128)} %bitcast.15), custom_call_target="tpu_custom_call" | custom-call | flops 4831838208 | bytes 6291456 | tf_op jit(solution)/shard_map/bags/pallas_call | solution.py:465
  97.0 2.6 %finish.1 = (f32[1,1,1024,256]{3,2,1,0:T(8,128)}, f32[1,1,1024]{2,1,0:T(1,128)}, f32[1,16,1,64,256]{4,3,2,1,0:T(8,128)}, f32[1,16,1,64]{3,2,1,0:T(1,128)}) custom-call(f32[1024,256]{1,0:T(8,128)} %get-tuple-element.8.table_hbm, f32[1,1024]{1,0:T(1,128)} %get-tuple-element.9.state_hbm, s16[16,64,256]{2,1,0:T(8,128)(2,1)} %get-tuple-element.10.code_hbm, ...), custom_call_target="tpu_custom_call" | custom-call | flops 262144 | bytes 2621440 | tf_op jit(solution)/shard_map/finish/pallas_call | solution.py:527

commit v5 on v4

--- a/solution.py
+++ b/solution.py
@@ -12,6 +12,7 @@
 PARTS = 2
 TOP = 32767.0
 VMEM_BYTES = 60 * 1024 * 1024
+SPOTS = (0, 1, 2, 3, 4, 5)
 
 learn_rate = 0.05
 epsilon = 1e-08
@@ -60,9 +61,6 @@
             (counts_hbm, counts_ref),
         ))
     ]
-    for load in loads:
-        load.start()
-
     def dest(k):
         return ((my_wing + 1 + k // wing) % 2) * wing + (my_place + k) % wing
 
@@ -82,6 +80,8 @@
 
     lax.fori_loop(1, shards, greet_shard, 0)
     lax.fori_loop(1, groups, greet_group, 0)
+    for load in loads:
+        load.start()
 
     def block_copy(source, target, send_sem, recv_sem, part, other):
         return pltpu.make_async_remote_copy(
@@ -109,14 +109,23 @@
             other = first + (my_spot + turn) % line
             block_copy(source, target, send_sem, recv_sem, part, other).start()
 
+    def send_spot(source, target, send_sem, recv_sem, part, spot):
+        def spot_step(step, carry):
+            other = ((my_line + step) % lines) * line + spot
+            copy = block_copy(source, target, send_sem, recv_sem, part, other)
+            pl.when(other != me)(copy.start)
+            return carry
+
+        lax.fori_loop(0, lines, spot_step, 0)
+
     loads[0].wait()
     loads[1].wait()
     slot = lax.broadcasted_iota(jnp.int32, (slots, samples), 0)
     live = jnp.where(slot < len_ref[...], ids_ref[...], -1)
     live = jnp.concatenate([live, jnp.full((8 - slots, samples), -1, jnp.int32)], axis=0)
-    columns = live.T.reshape(shards, PARTS, deep, 8)
+    columns = live.T.reshape(lines, line, PARTS, deep, 8)
     for part in range(PARTS):
-        ids_col[part] = columns[:, part]
+        ids_col[part] = columns[:, :, part]
 
     loads[2].wait()
     high, middle, low = split_three(table_ref[...])
@@ -124,32 +133,45 @@
     parts[:, width:2 * width] = middle
     parts[:, 2 * width:3 * width] = low
 
-    def pool_line(part, step):
-        first = ((my_line + step) % lines) * line
-        column = ids_col[part, pl.ds(first, line)].reshape(line * deep, 8)
-        lane = lax.broadcasted_iota(jnp.int32, (line * deep, rows), 1)
-        total = jnp.zeros((line * deep, rows), jnp.float32)
+    def pool(column):
+        lane = lax.broadcasted_iota(jnp.int32, (column.shape[0], rows), 1)
+        total = jnp.zeros((column.shape[0], rows), jnp.float32)
         for j in range(slots):
             total = total + jnp.where(column[:, j:j + 1] == lane, 1.0, 0.0)
         product = jnp.dot(
             total.astype(jnp.bfloat16), parts[...], preferred_element_type=jnp.float32
         )
         pooled = product[:, 0:width] + product[:, width:2 * width]
-        pooled = pooled + product[:, 2 * width:3 * width]
-        send1[part, pl.ds(first, line)] = pooled.astype(jnp.bfloat16).reshape(line, deep, width)
-
-    for part in range(PARTS):
-        def pool_step(step, carry, part=part):
-            pool_line(part, step)
-            send_line(send1, recv1, send1_sem, recv1_sem, part, step, 0)
-            return carry
-
-        pool_line(part, 0)
-        if part == 0:
-            pl.semaphore_wait(barrier, shards + groups - 2)
-        send_line(send1, recv1, send1_sem, recv1_sem, part, 0, 1)
-        lax.fori_loop(1, lines, pool_step, 0)
-        recv1[part, me] = send1[part, me]
+        return (pooled + product[:, 2 * width:3 * width]).astype(jnp.bfloat16)
+
+    def pool_line(part, step):
+        at = (my_line + step) % lines
+        pooled = pool(ids_col[part, at].reshape(line * deep, 8))
+        send1[part, pl.ds(at * line, line)] = pooled.reshape(line, deep, width)
+
+    def pool_spot(part, spot):
+        pooled = pool(ids_col[part, :, spot].reshape(lines * deep, 8))
+        for at in range(lines):
+            send1[part, at * line + spot] = pooled[at * deep:(at + 1) * deep]
+
+    def first_step(step, carry):
+        pool_line(0, step)
+        send_line(send1, recv1, send1_sem, recv1_sem, 0, step, 0)
+        return carry
+
+    pool_line(0, 0)
+    pl.semaphore_wait(barrier, shards + groups - 2)
+    send_line(send1, recv1, send1_sem, recv1_sem, 0, 0, 1)
+    lax.fori_loop(1, lines, first_step, 0)
+    recv1[0, me] = send1[0, me]
+
+    def second_step(spot, carry):
+        pool_spot(1, spot)
+        send_spot(send1, recv1, send1_sem, recv1_sem, 1, spot)
+        return carry
+
+    lax.fori_loop(0, line, second_step, 0)
+    recv1[1, me] = send1[1, me]
 
     loads[3].wait()
 
@@ -183,26 +205,8 @@
         both = jnp.concatenate([out_left[...], out_right[...]], axis=1)
         send2[part] = both.astype(jnp.bfloat16).reshape(shards, deep, width)
 
-        def back_step(step, carry):
-            if part == 0:
-                send_line(send2, recv2, send2_sem, recv2_sem, part, step, 0)
-                return carry
-            odd = step // lines
-            first = ((my_line + step) % lines) * line
-            for turn in range(line // 2):
-                other = first + ((my_spot // 2 + turn) % (line // 2)) * 2 + odd
-                copy = block_copy(send2, recv2, send2_sem, recv2_sem, part, other)
-                if turn == 0:
-                    pl.when(other != me)(copy.start)
-                else:
-                    copy.start()
-            return carry
-
-        if part == 0:
-            send_line(send2, recv2, send2_sem, recv2_sem, part, 0, 1)
-            lax.fori_loop(1, lines, back_step, 0)
-        else:
-            lax.fori_loop(0, 2 * lines, back_step, 0)
+        for spot in SPOTS if line == 6 else range(line):
+            send_spot(send2, recv2, send2_sem, recv2_sem, part, spot)
         recv2[part, me] = send2[part, me]
 
     mix_part(0)
@@ -480,7 +484,7 @@
             pltpu.VMEM((1, samples), i32),
             pltpu.VMEM((samples, shards), f32),
             pltpu.SMEM((1, groups), i32),
-            pltpu.VMEM((PARTS, shards, deep, 8), i32),
+            pltpu.VMEM((PARTS, shards // line, line, deep, 8), i32),
             pltpu.VMEM((8, samples), i32),
             pltpu.VMEM((rows, 3 * width), bf16),
             pltpu.VMEM((rows, 128), bf16),

time: 99.8 us -> 96.2 us (0.964)
  the two profiles are of different devices: /device:TPU:1 before, /device:TPU:129 now
where the time goes in v5:
time: 96.2 us; the launch traced here: 96 us
  Pallas kernels  95.3 us (99%)
    pallas_call x1, Pallas kernels, on_device(): pl.pallas_call(functools.partial(bag_kernel, groups, shards, line), name=...  92.8 us
    pallas_call x1, Pallas kernels, on_device(): pl.pallas_call(finish_kernel, name='finish', out_shape=(jax.ShapeDtypeStr...  2.57 us

profile of v5, /device:TPU:129, one launch (start us, length us, event | category | flops | bytes accessed | tf_op | source)
XLA Modules:
  0.0 96.0 jit_solution(6774291961141266093)
XLA Ops:
  0.6 92.8 %bags.1 = (f32[1024,256]{1,0:T(8,128)}, f32[1,1024]{1,0:T(1,128)}, s16[16,64,256]{2,1,0:T(8,128)(2,1)}, f32[16,2,128]{2,1,0:T(2,128)}) custom-call(f32[1024,256]{1,0:T(8,128)} %bitcast.10, f32[1,1024]{1,0:T(1,128)} %bitcast.14, s32[4,1536]{1,0:T(4,128)} %bitcast.12, s32[1,1536]{1,0:T(1,128)} %bitcast.13, f32[1536,48]{1,0:T(8,128)} %bitcast.11, s32[1,16]{1,0:T(1,128)} %bitcast.15), custom_call_target="tpu_custom_call" | custom-call | flops 4831838208 | bytes 6291456 | tf_op jit(solution)/shard_map/bags/pallas_call | solution.py:469
  93.4 2.6 %finish.1 = (f32[1,1,1024,256]{3,2,1,0:T(8,128)}, f32[1,1,1024]{2,1,0:T(1,128)}, f32[1,16,1,64,256]{4,3,2,1,0:T(8,128)}, f32[1,16,1,64]{3,2,1,0:T(1,128)}) custom-call(f32[1024,256]{1,0:T(8,128)} %get-tuple-element.8.table_hbm, f32[1,1024]{1,0:T(1,128)} %get-tuple-element.9.state_hbm, s16[16,64,256]{2,1,0:T(8,128)(2,1)} %get-tuple-element.10.code_hbm, ...), custom_call_target="tpu_custom_call" | custom-call | flops 262144 | bytes 2621440 | tf_op jit(solution)/shard_map/finish/pallas_call | solution.py:531

commit v6 on v5

--- a/solution.py
+++ b/solution.py
@@ -12,7 +12,7 @@
 PARTS = 2
 TOP = 32767.0
 VMEM_BYTES = 60 * 1024 * 1024
-SPOTS = (0, 1, 2, 3, 4, 5)
+SPOTS = (0, 1, 2, 3, 5, 4)
 
 learn_rate = 0.05
 epsilon = 1e-08

time: 96.2 us -> 94.6 us (0.983)
  the two profiles are of different devices: /device:TPU:129 before, /device:TPU:64 now
where the time goes in v6:
time: 94.6 us; the launch traced here: 94.4 us
  Pallas kernels  93.8 us (99%)
    pallas_call x1, Pallas kernels, on_device(): pl.pallas_call(functools.partial(bag_kernel, groups, shards, line), name=...  91.2 us
    pallas_call x1, Pallas kernels, on_device(): pl.pallas_call(finish_kernel, name='finish', out_shape=(jax.ShapeDtypeStr...  2.57 us

profile of v6, /device:TPU:64, one launch (start us, length us, event | category | flops | bytes accessed | tf_op | source)
XLA Modules:
  0.0 94.4 jit_solution(11291048915148719212)
XLA Ops:
  0.6 91.2 %bags.1 = (f32[1024,256]{1,0:T(8,128)}, f32[1,1024]{1,0:T(1,128)}, s16[16,64,256]{2,1,0:T(8,128)(2,1)}, f32[16,2,128]{2,1,0:T(2,128)}) custom-call(f32[1024,256]{1,0:T(8,128)} %bitcast.10, f32[1,1024]{1,0:T(1,128)} %bitcast.14, s32[4,1536]{1,0:T(4,128)} %bitcast.12, s32[1,1536]{1,0:T(1,128)} %bitcast.13, f32[1536,48]{1,0:T(8,128)} %bitcast.11, s32[1,16]{1,0:T(1,128)} %bitcast.15), custom_call_target="tpu_custom_call" | custom-call | flops 4831838208 | bytes 6291456 | tf_op jit(solution)/shard_map/bags/pallas_call | solution.py:469
  91.8 2.6 %finish.1 = (f32[1,1,1024,256]{3,2,1,0:T(8,128)}, f32[1,1,1024]{2,1,0:T(1,128)}, f32[1,16,1,64,256]{4,3,2,1,0:T(8,128)}, f32[1,16,1,64]{3,2,1,0:T(1,128)}) custom-call(f32[1024,256]{1,0:T(8,128)} %get-tuple-element.8.table_hbm, f32[1,1024]{1,0:T(1,128)} %get-tuple-element.9.state_hbm, s16[16,64,256]{2,1,0:T(8,128)(2,1)} %get-tuple-element.10.code_hbm, ...), custom_call_target="tpu_custom_call" | custom-call | flops 262144 | bytes 2621440 | tf_op jit(solution)/shard_map/finish/pallas_call | solution.py:531

commit v7 on v6

--- a/solution.py
+++ b/solution.py
@@ -47,7 +47,6 @@
     my_line = me // line
     my_spot = me % line
     wing = groups // 2
-    my_wing = group // wing
     my_place = group % wing
 
     loads = [
@@ -62,7 +61,7 @@
         ))
     ]
     def dest(k):
-        return ((my_wing + 1 + k // wing) % 2) * wing + (my_place + k) % wing
+        return (k // wing) * wing + (my_place + k) % wing
 
     barrier = pltpu.get_barrier_semaphore()
 
@@ -330,7 +329,7 @@
             code_send[other] = values[turn]
             side_send[other, :, 0:CAP] = aside[0:2, turn * CAP:(turn + 1) * CAP]
 
-            @pl.when(k != wing)
+            @pl.when(other != group)
             def _():
                 code_copy(other).start()
                 side_copy(other).start()

time: 94.6 us -> 96.3 us (1.018)
  the two profiles are of different devices: /device:TPU:64 before, /device:TPU:2 now
where the time goes in v7:
time: 96.3 us; the launch traced here: 96.1 us
  Pallas kernels  95.5 us (99%)
    pallas_call x1, Pallas kernels, on_device(): pl.pallas_call(functools.partial(bag_kernel, groups, shards, line), name=...  92.9 us
    pallas_call x1, Pallas kernels, on_device(): pl.pallas_call(finish_kernel, name='finish', out_shape=(jax.ShapeDtypeStr...  2.57 us

profile of v7, /device:TPU:2, one launch (start us, length us, event | category | flops | bytes accessed | tf_op | source)
XLA Modules:
  0.0 96.1 jit_solution(4756435073514035075)
XLA Ops:
  0.6 92.9 %bags.1 = (f32[1024,256]{1,0:T(8,128)}, f32[1,1024]{1,0:T(1,128)}, s16[16,64,256]{2,1,0:T(8,128)(2,1)}, f32[16,2,128]{2,1,0:T(2,128)}) custom-call(f32[1024,256]{1,0:T(8,128)} %bitcast.10, f32[1,1024]{1,0:T(1,128)} %bitcast.14, s32[4,1536]{1,0:T(4,128)} %bitcast.12, s32[1,1536]{1,0:T(1,128)} %bitcast.13, f32[1536,48]{1,0:T(8,128)} %bitcast.11, s32[1,16]{1,0:T(1,128)} %bitcast.15), custom_call_target="tpu_custom_call" | custom-call | flops 4831838208 | bytes 6291456 | tf_op jit(solution)/shard_map/bags/pallas_call | solution.py:468
  93.5 2.6 %finish.1 = (f32[1,1,1024,256]{3,2,1,0:T(8,128)}, f32[1,1,1024]{2,1,0:T(1,128)}, f32[1,16,1,64,256]{4,3,2,1,0:T(8,128)}, f32[1,16,1,64]{3,2,1,0:T(1,128)}) custom-call(f32[1024,256]{1,0:T(8,128)} %get-tuple-element.8.table_hbm, f32[1,1024]{1,0:T(1,128)} %get-tuple-element.9.state_hbm, s16[16,64,256]{2,1,0:T(8,128)(2,1)} %get-tuple-element.10.code_hbm, ...), custom_call_target="tpu_custom_call" | custom-call | flops 262144 | bytes 2621440 | tf_op jit(solution)/shard_map/finish/pallas_call | solution.py:530
